TPU v7x, 512 devices: a whole 4x8x8 slice. The times are simulated.
512 devices in a mesh: gx: 32 (over z, x), gy: 16 (over y, core).
Axes of the slice: x: 4, y: 8, z: 8, core: 2. Of those that a mesh axis runs over, the one named last changes fastest.
Arguments:
- state: float32 [12, 96, 131072], P(None, None, ('gx', 'gy')), may hold values from -6 to 6
- events: int32 [8, 131072], P(None, ('gx', 'gy')), may hold values 0 or 1
- event_embed: float32 [96], replicated, may hold values from -4 to 4
- gains: float32 [3, 96], replicated, may hold values from 0.5 to 1.5
- taps_t: float32 [96, 9], replicated, may hold values from -2 to 2
- taps_y: float32 [96, 33], replicated, may hold values from -1 to 1
- taps_x: float32 [96, 33], replicated, may hold values from -1 to 1
- mixers: float32 [3, 2, 96, 96], replicated, may hold values from -0.625 to 0.625
Outputs:
- result: float32 [12, 96, 131072], P(None, None, ('gx', 'gy'))
All inputs are finite; a program needn't handle non-finite values. No bound on the sum of `events` on one device may be relied on, other than what follows from the above.
Results may differ from a plain program's by a relative error of at most 0.0003.
Values sent between devices are 32-bit elements; how exact they have to be, the bound alone decides.
No kernel may reach another device: no remote copies, remote signals or barrier semaphores. Data moves between devices by JAX's collectives and lax.ppermute only.
A program may use at most 128 MiB of HBM per device.

v0:
```python
import jax
import jax.numpy as jnp
from jax import lax
from jax.sharding import PartitionSpec as P

X_DEV = 16
Y_DEV = 16


def padded_2(cells, sides, width):
    for axis, dim in sides:
        count = lax.axis_size(axis)
        ends = count - 1
        head = lax.slice_in_dim(cells, 0, width, axis=dim)
        tail = lax.slice_in_dim(cells, cells.shape[dim] - width, cells.shape[dim], axis=dim)
        cells = jnp.concatenate(
            [
                lax.ppermute(tail, axis, [(i, (i + 1) % count) for i in range(ends)]),
                cells,
                lax.ppermute(head, axis, [((i + 1) % count, i) for i in range(ends)]),
            ],
            axis=dim,
        )
    return cells


def normed(field, gain):
    meansq = jnp.mean(field * field, axis=1, keepdims=True)
    return field * lax.rsqrt(meansq + 1e-06) * gain[None, :, None, None]


def mixed(field, conv, weights):
    value = jnp.einsum("oc,rcxy->roxy", weights[0], conv, precision=lax.Precision.HIGHEST)
    gate = jnp.einsum("oc,rcxy->roxy", weights[1], conv, precision=lax.Precision.HIGHEST)
    return field + value * jax.nn.sigmoid(gate)


def tap_sum(padded, taps, axis, width):
    conv = jnp.zeros(padded.shape[:axis] + (width,) + padded.shape[axis + 1 :], jnp.float32)
    for k in range(taps.shape[1]):
        piece = lax.slice_in_dim(padded, k, k + width, axis=axis)
        conv = conv + taps[:, k][None, :, None, None] * piece
    return conv


def local(state, events, event_embed, gains, taps_t, taps_y, taps_x, mixers):
    rounds = state.shape[0]
    channels = state.shape[1]
    rows_here = X_DEV
    cols_here = Y_DEV
    half = taps_y.shape[1] // 2
    block_state = state.reshape(rounds, channels, rows_here, cols_here)
    block_events = events.reshape(events.shape[0], rows_here, cols_here)
    history = (
        event_embed[None, :, None, None] * (2.0 * block_events.astype(jnp.float32) - 1.0)[:, None]
    )
    extended = jnp.concatenate([history, normed(block_state, gains[0])], axis=0)
    conv_t = tap_sum(extended, taps_t, 0, rounds)
    first = mixed(block_state, conv_t, mixers[0])
    source_y = normed(first, gains[1])
    padded_y = padded_2(source_y, (("gy", 3),), half)
    conv_y = tap_sum(padded_y, taps_y, 3, cols_here)
    second = mixed(first, conv_y, mixers[1])
    source_x = normed(second, gains[2])
    padded_x = padded_2(source_x, (("gx", 2),), half)
    conv_x = tap_sum(padded_x, taps_x, 2, rows_here)
    final = mixed(second, conv_x, mixers[2])
    return final.reshape(rounds, channels, rows_here * cols_here)


def solution(mesh):
    placed = (P(None, None, ("gx", "gy")), P(None, ("gx", "gy")), P(), P(), P(), P(), P(), P())
    return jax.shard_map(
        local, mesh=mesh, in_specs=placed, out_specs=P(None, None, ("gx", "gy")), check_vma=False
    )
```

profile of v0, /device:TPU:238, one launch (start us, length us, event | category | flops | bytes accessed | tf_op | source)
XLA Modules:
  0.0 132.2 jit_solution(17013009483874089086)
XLA Ops:
  0.0 1.8 %copy.9 = f32[12,96,256]{1,2,0:T(8,128)S(1)} copy(f32[12,96,256]{2,1,0:T(8,128)} %param.8) | data formatting | bytes 2359296 | tf_op args[0]
  3.6 1.7 %fusion.4 = f32[12,96,16,16]{1,3,2,0:T(8,128)S(1)} fusion(f32[12,96,16,16]{1,3,2,0:T(8,128)S(1)} %multiply_multiply_fusion.2, f32[8,96,16,16]{1,3,2,0:T(8,128)S(1)} %broadcast_multiply_fusion, f32[96]{0:T(128)S(1)} %get-tuple-element.78, f32[96]{0:T(128)S(1)} %get-tuple-element.79, f32[96]{0:T(128)S(1)} %get-tuple-element.72, f32[96]{0:T(128)S(1)} %get-tuple-element.73, ...), kind=kLoop, calls=%fused_computation.130 | loop fusion | flops 7372800 | bytes 3149184 | tf_op jit(solution)/shard_map/add | solution.py:42
  5.3 1.4 %fusion.210 = f32[12,16,16,96]{3,2,1,0:T(8,128)S(1)} fusion(f32[12,96,16,16]{1,3,2,0:T(8,128)S(1)} %fusion.4, f32[3,2,96,96]{3,2,1,0:T(8,128)S(1)} %copy-done.7), kind=kOutput, calls=%fused_computation.353 | convolution fusion | flops 339738624 | bytes 2801664 | tf_op jit(solution)/shard_map/oc,rcxy->roxy/dot_general | solution.py:33
  6.7 1.9 %multiply_reduce_fusion.1 = (f32[12,16,16]{2,1,0:T(8,128)S(1)}, f32[12,96,16,16]{1,3,2,0:T(8,128)S(1)}) fusion(f32[12,96,16,16]{1,3,2,0:T(8,128)S(1)} %bitcast.217, f32[12,16,16,96]{3,2,1,0:T(8,128)S(1)} %fusion.210, f32[12,96,16,16]{1,3,2,0:T(8,128)S(1)} %fusion.4, f32[3,2,96,96]{3,2,1,0:T(8,128)S(1)} %copy-done.7), kind=kOutput, calls=%fused_computation.340 | convolution fusion | flops 341799936 | bytes 5959680 | tf_op jit(solution)/shard_map/oc,rcxy->roxy/dot_general | solution.py:34
  9.1 0.6 copy-done.1
  9.8 1.9 %collective-permute-start = (f32[12,96,16,16]{1,3,2,0:T(8,128)S(1)}, f32[12,96,16,16]{1,3,2,0:T(8,128)S(1)}, u32[]{:S(2)}, u32[]{:S(2)}) collective-permute-start(f32[12,96,16,16]{1,3,2,0:T(8,128)S(1)} %multiply_multiply_fusion.1), channel_id=1, source_target_pairs={{0,1},{1,2},{2,3},{3,4},{4,5},{5,6},{6,7},{7,8},{8,9},{9,10},{10,1... | collective-permute-start | bytes 3538952 | tf_op jit(solution)/shard_map/ppermute | solution.py:18
  11.7 3.8 %collective-permute-start.1 = (f32[12,96,16,16]{1,3,2,0:T(8,128)S(1)}, f32[12,96,16,16]{1,3,2,0:T(8,128)S(1)}, u32[]{:S(2)}, u32[]{:S(2)}) collective-permute-start(f32[12,96,16,16]{1,3,2,0:T(8,128)S(1)} %multiply_multiply_fusion.1), channel_id=1, source_target_pairs={{1,0},{2,1},{3,2},{4,3},{5,4},{6,5},{7,6},{8,7},{9,8},{10,9},{11,1... | collective-permute-start | bytes 3538952 | tf_op jit(solution)/shard_map/ppermute | solution.py:20
  15.5 0.6 slice_bitcast_fusion.67
  16.1 15.3 %collective-permute-done = f32[12,96,16,16]{1,3,2,0:T(8,128)S(1)} collective-permute-done((f32[12,96,16,16]{1,3,2,0:T(8,128)S(1)}, f32[12,96,16,16]{1,3,2,0:T(8,128)S(1)}, u32[]{:S(2)}, u32[]{:S(2)}) %collective-permute-start) | collective-permute-done | bytes 1179680 | tf_op jit(solution)/shard_map/ppermute | solution.py:18
  31.5 1.8 %collective-permute-done.1 = f32[12,96,16,16]{1,3,2,0:T(8,128)S(1)} collective-permute-done((f32[12,96,16,16]{1,3,2,0:T(8,128)S(1)}, f32[12,96,16,16]{1,3,2,0:T(8,128)S(1)}, u32[]{:S(2)}, u32[]{:S(2)}) %collective-permute-start.1) | collective-permute-done | bytes 1179680 | tf_op jit(solution)/shard_map/ppermute | solution.py:20
  33.3 1.1 copy-done.5
  34.4 23.7 %fusion.114 = f32[12,96,16,16]{1,3,2,0:T(8,128)S(1)} fusion(f32[12,96,16,16]{1,3,2,0:T(8,128)S(1)} %multiply_multiply_fusion.1, f32[12,96,16,16]{1,3,2,0:T(8,128)} %copy-done.5, f32[12,96,16,16]{1,3,2,0:T(8,128)} %copy-done.3, f32[96]{0:T(128)S(1)} %get-tuple-element.69, f32[96]{0:T(128)S(1)} %get-tuple-element.70, f32[96]{0:T(128)S(1)} %get-tuple-element.39, ...), kind=kLoop, calls=%fused_computation.240 | loop fusion | flops 28016640 | bytes 4731264 | tf_op jit(solution)/shard_map/add | solution.py:42
  58.1 1.4 %fusion.206 = f32[12,16,16,96]{3,2,1,0:T(8,128)S(1)} fusion(f32[12,96,16,16]{1,3,2,0:T(8,128)S(1)} %fusion.114, f32[3,2,96,96]{3,2,1,0:T(8,128)S(1)} %copy-done.7), kind=kOutput, calls=%fused_computation.349 | convolution fusion | flops 339738624 | bytes 2801664 | tf_op jit(solution)/shard_map/oc,rcxy->roxy/dot_general | solution.py:34
  59.5 1.8 %multiply_reduce_fusion = (f32[12,16,16]{2,1,0:T(8,128)S(1)}, f32[12,96,16,16]{1,3,2,0:T(8,128)S(1)}) fusion(f32[12,96,16,16]{1,3,2,0:T(8,128)S(1)} %copy-done.2, f32[12,16,16,96]{3,2,1,0:T(8,128)S(1)} %fusion.206, f32[12,96,16,16]{1,3,2,0:T(8,128)S(1)} %fusion.114, f32[3,2,96,96]{3,2,1,0:T(8,128)S(1)} %copy-done.7), kind=kOutput, calls=%fused_computation.338 | convolution fusion | flops 341799936 | bytes 5959680 | tf_op jit(solution)/shard_map/oc,rcxy->roxy/dot_general | solution.py:33
  61.9 5.4 %collective-permute-start.2 = (f32[12,96,16,16]{1,3,2,0:T(8,128)S(1)}, f32[12,96,16,16]{1,3,2,0:T(8,128)S(1)}, u32[]{:S(2)}, u32[]{:S(2)}) collective-permute-start(f32[12,96,16,16]{1,3,2,0:T(8,128)S(1)} %multiply_multiply_fusion), channel_id=1, source_target_pairs={{0,16},{16,32},{32,48},{48,64},{64,80},{80,96},{96,112},{112,128},... | collective-permute-start | bytes 3538952 | tf_op jit(solution)/shard_map/ppermute | solution.py:18
  67.3 2.1 %collective-permute-start.3 = (f32[12,96,16,16]{1,3,2,0:T(8,128)S(1)}, f32[12,96,16,16]{1,3,2,0:T(8,128)S(1)}, u32[]{:S(2)}, u32[]{:S(2)}) collective-permute-start(f32[12,96,16,16]{1,3,2,0:T(8,128)S(1)} %multiply_multiply_fusion), channel_id=1, source_target_pairs={{16,0},{32,16},{48,32},{64,48},{80,64},{96,80},{112,96},{128,112},... | collective-permute-start | bytes 3538952 | tf_op jit(solution)/shard_map/ppermute | solution.py:20
  69.5 0.6 slice_bitcast_fusion.33
  70.1 32.0 %collective-permute-done.2 = f32[12,96,16,16]{1,3,2,0:T(8,128)S(1)} collective-permute-done((f32[12,96,16,16]{1,3,2,0:T(8,128)S(1)}, f32[12,96,16,16]{1,3,2,0:T(8,128)S(1)}, u32[]{:S(2)}, u32[]{:S(2)}) %collective-permute-start.2) | collective-permute-done | bytes 1179680 | tf_op jit(solution)/shard_map/ppermute | solution.py:18
  102.1 7.4 %collective-permute-done.3 = f32[12,96,16,16]{1,3,2,0:T(8,128)S(1)} collective-permute-done((f32[12,96,16,16]{1,3,2,0:T(8,128)S(1)}, f32[12,96,16,16]{1,3,2,0:T(8,128)S(1)}, u32[]{:S(2)}, u32[]{:S(2)}) %collective-permute-start.3) | collective-permute-done | bytes 1179680 | tf_op jit(solution)/shard_map/ppermute | solution.py:20
  109.5 1.2 copy-done.6
  110.7 14.4 %fusion.26 = f32[12,96,16,16]{1,3,2,0:T(8,128)S(1)} fusion(f32[12,96,16,16]{1,3,2,0:T(8,128)S(1)} %multiply_multiply_fusion, f32[12,96,16,16]{1,3,2,0:T(8,128)} %copy-done.6, f32[12,96,16,16]{1,3,2,0:T(8,128)} %copy-done.4, f32[96]{0:T(128)S(1)} %get-tuple-element.36, f32[96]{0:T(128)S(1)} %get-tuple-element.37, f32[96]{0:T(128)S(1)} %get-tuple-element.6, ...), kind=kLoop, calls=%fused_computation.152 | loop fusion | flops 28016640 | bytes 4731264 | tf_op jit(solution)/shard_map/add | solution.py:42
  125.1 1.4 %fusion.203 = f32[12,16,16,96]{3,2,1,0:T(8,128)S(1)} fusion(f32[12,96,16,16]{1,3,2,0:T(8,128)S(1)} %fusion.26, f32[3,2,96,96]{3,2,1,0:T(8,128)S(1)} %copy-done.7), kind=kOutput, calls=%fused_computation.346 | convolution fusion | flops 339738624 | bytes 2801664 | tf_op jit(solution)/shard_map/oc,rcxy->roxy/dot_general | solution.py:34
  126.6 2.7 %bitcast_add_fusion = f32[12,96,16,16]{1,3,2,0:T(8,128)} fusion(f32[12,96,16,16]{1,3,2,0:T(8,128)S(1)} %get-tuple-element.86, f32[12,16,16,96]{3,2,1,0:T(8,128)S(1)} %fusion.203, f32[12,96,16,16]{1,3,2,0:T(8,128)S(1)} %fusion.26, f32[3,2,96,96]{3,2,1,0:T(8,128)S(1)} %copy-done.7), kind=kOutput, calls=%fused_computation.334 | convolution fusion | flops 341213184 | bytes 5947392 | tf_op jit(solution)/shard_map/oc,rcxy->roxy/dot_general | solution.py:33
  129.3 2.9 %copy.10 = f32[12,96,256]{2,1,0:T(8,128)} copy(f32[12,96,256]{1,2,0:T(8,128)} %bitcast.218) | data formatting | bytes 2359296 | tf_op jit(solution)/shard_map/reshape | solution.py:68
  (42 shorter events, 2.7 us)
Async XLA Ops:
  0.0 1.9 %copy-start = (f32[12,96,256]{2,1,0:T(8,128)S(1)}, f32[12,96,256]{2,1,0:T(8,128)}, u32[]{:S(2)}) copy-start(f32[12,96,256]{2,1,0:T(8,128)} %param.8) | copy-start | bytes 3538948
  0.0 2.0 %copy-start.11 = (f32[96,9]{0,1:T(8,128)S(1)}, f32[96,9]{0,1:T(8,128)}, u32[]{:S(2)}) copy-start(f32[96,9]{0,1:T(8,128)} %param.12) | copy-start | bytes 10372
  0.0 2.0 %copy-start.13 = (f32[3,96]{1,0:T(4,128)S(1)}, f32[3,96]{1,0:T(4,128)}, u32[]{:S(2)}) copy-start(f32[3,96]{1,0:T(4,128)} %param.11) | copy-start | bytes 3460
  0.0 2.6 %copy-start.10 = (s32[8,256]{1,0:T(8,128)S(1)}, s32[8,256]{1,0:T(8,128)}, u32[]{:S(2)}) copy-start(s32[8,256]{1,0:T(8,128)} %param.9) | copy-start | bytes 24580
  0.0 2.7 %copy-start.14 = (f32[96]{0:T(128)S(1)}, f32[96]{0:T(128)}, u32[]{:S(2)}) copy-start(f32[96]{0:T(128)} %param.10) | copy-start | bytes 1156
  3.6 1.7 %copy-start.7 = (f32[3,2,96,96]{3,2,1,0:T(8,128)S(1)}, f32[3,2,96,96]{3,2,1,0:T(8,128)}, u32[]{:S(2)}) copy-start(f32[3,2,96,96]{3,2,1,0:T(8,128)} %param.15) | copy-start | bytes 663556
  8.6 1.2 copy-start.1
  8.6 6.9 %copy-start.8 = (f32[96,33]{0,1:T(8,128)S(1)}, f32[96,33]{0,1:T(8,128)}, u32[]{:S(2)}) copy-start(f32[96,33]{0,1:T(8,128)} %param.13) | copy-start | bytes 38020
  9.8 21.7 %collective-permute-start = (f32[12,96,16,16]{1,3,2,0:T(8,128)S(1)}, f32[12,96,16,16]{1,3,2,0:T(8,128)S(1)}, u32[]{:S(2)}, u32[]{:S(2)}) collective-permute-start(f32[12,96,16,16]{1,3,2,0:T(8,128)S(1)} %multiply_multiply_fusion.1), channel_id=1, source_target_pairs={{0,1},{1,2},{2,3},{3,4},{4,5},{5,6},{6,7},{7,8},{8,9},{9,10},{10,1... | collective-permute-start | bytes 3538952 | tf_op jit(solution)/shard_map/ppermute | solution.py:18
  11.7 21.6 %collective-permute-start.1 = (f32[12,96,16,16]{1,3,2,0:T(8,128)S(1)}, f32[12,96,16,16]{1,3,2,0:T(8,128)S(1)}, u32[]{:S(2)}, u32[]{:S(2)}) collective-permute-start(f32[12,96,16,16]{1,3,2,0:T(8,128)S(1)} %multiply_multiply_fusion.1), channel_id=1, source_target_pairs={{1,0},{2,1},{3,2},{4,3},{5,4},{6,5},{7,6},{8,7},{9,8},{10,9},{11,1... | collective-permute-start | bytes 3538952 | tf_op jit(solution)/shard_map/ppermute | solution.py:20
  31.5 1.8 %copy-start.3 = (f32[12,96,16,16]{1,3,2,0:T(8,128)}, f32[12,96,16,16]{1,3,2,0:T(8,128)S(1)}, u32[]{:S(2)}) copy-start(f32[12,96,16,16]{1,3,2,0:T(8,128)S(1)} %collective-permute-done) | copy-start | bytes 3538948
  33.3 1.1 copy-start.5
  58.1 1.5 %copy-start.2 = (f32[12,96,16,16]{1,3,2,0:T(8,128)S(1)}, f32[12,96,16,16]{1,3,2,0:T(8,128)}, u32[]{:S(2)}) copy-start(f32[12,96,16,16]{1,3,2,0:T(8,128)} %copy-done.1) | copy-start | bytes 3538948
  59.5 1.9 %copy-start.12 = (f32[96]{0:T(128)S(1)}, f32[96]{0:T(128)}, u32[]{:S(2)}) copy-start(f32[96]{0:T(128)} %get-tuple-element.80) | copy-start | bytes 1156
  61.4 8.1 %copy-start.9 = (f32[96,33]{0,1:T(8,128)S(1)}, f32[96,33]{0,1:T(8,128)}, u32[]{:S(2)}) copy-start(f32[96,33]{0,1:T(8,128)} %param.14) | copy-start | bytes 38020
  61.9 40.2 %collective-permute-start.2 = (f32[12,96,16,16]{1,3,2,0:T(8,128)S(1)}, f32[12,96,16,16]{1,3,2,0:T(8,128)S(1)}, u32[]{:S(2)}, u32[]{:S(2)}) collective-permute-start(f32[12,96,16,16]{1,3,2,0:T(8,128)S(1)} %multiply_multiply_fusion), channel_id=1, source_target_pairs={{0,16},{16,32},{32,48},{48,64},{64,80},{80,96},{96,112},{112,128},... | collective-permute-start | bytes 3538952 | tf_op jit(solution)/shard_map/ppermute | solution.py:18
  67.3 42.2 %collective-permute-start.3 = (f32[12,96,16,16]{1,3,2,0:T(8,128)S(1)}, f32[12,96,16,16]{1,3,2,0:T(8,128)S(1)}, u32[]{:S(2)}, u32[]{:S(2)}) collective-permute-start(f32[12,96,16,16]{1,3,2,0:T(8,128)S(1)} %multiply_multiply_fusion), channel_id=1, source_target_pairs={{16,0},{32,16},{48,32},{64,48},{80,64},{96,80},{112,96},{128,112},... | collective-permute-start | bytes 3538952 | tf_op jit(solution)/shard_map/ppermute | solution.py:20
  102.1 7.4 %copy-start.4 = (f32[12,96,16,16]{1,3,2,0:T(8,128)}, f32[12,96,16,16]{1,3,2,0:T(8,128)S(1)}, u32[]{:S(2)}) copy-start(f32[12,96,16,16]{1,3,2,0:T(8,128)S(1)} %collective-permute-done.2) | copy-start | bytes 3538948
  109.5 1.2 copy-start.6
where the time goes:
time: 133 us; the launch traced here: 132 us
  waiting for transfers between devices  56.5 us (42%)
  other arithmetic  41.7 us (31%)
  starting transfers between devices  13.3 us (10%)
  matrix products  10.7 us (8%)
  local copies, waits for them, and re-layouts  9.6 us (7%)
    ppermute x2, waiting for transfers between devices, padded_2(): lax.ppermute(tail, axis, [(i, (i + 1) % count) for i in range(ends)])  47.3 us
    add x3, other arithmetic, tap_sum(): conv = conv + taps[:, k][None, :, None, None] * piece  39.8 us
    ppermute x2, waiting for transfers between devices, padded_2(): lax.ppermute(head, axis, [((i + 1) % count, i) for i in range(ends)])  9.17 us
    ppermute x2, starting transfers between devices, padded_2(): lax.ppermute(tail, axis, [(i, (i + 1) % count) for i in range(ends)])  7.31 us
    dot_general x3, matrix products, mixed(): jnp.einsum('oc,rcxy->roxy', weights[0], conv, precision=lax.Precision.HIG...  5.99 us
    ppermute x2, starting transfers between devices, padded_2(): lax.ppermute(head, axis, [((i + 1) % count, i) for i in range(ends)])  5.96 us
    unnamed x31, local copies, waits for them, and re-layouts  4.82 us
    dot_general x3, matrix products, mixed(): jnp.einsum('oc,rcxy->roxy', weights[1], conv, precision=lax.Precision.HIG...  4.73 us
  transfers between devices with their start and end apart: 4, of which 4 were waited for; matrix products, arithmetic and copies ran while one was open for 1% of the time, Pallas kernels for 0%

commit v1 on v0

v1 whole, which is shorter than its diff:
```python
import functools

import jax
import jax.numpy as jnp
import numpy as np
from jax import lax
from jax.experimental import pallas as pl
from jax.experimental.pallas import tpu as pltpu
from jax.sharding import PartitionSpec as P

C = 96
ROUNDS = 12
SITES = 256
LANES = 128
HALF = 16
HIST = 8
KT = 9
CHUNK = 6
VMEM = 20 * 1024 * 1024


def lane_orders():
    x, y = np.divmod(np.arange(SITES), 16)
    native = x * 16 + y
    along_y = (x // 8) * 128 + y * 8 + x % 8
    along_x = (y // 8) * 128 + x * 8 + y % 8
    return native, along_y, along_x


def moving(source, target):
    matrix = np.zeros((SITES, SITES), np.float32)
    matrix[source, target] = 1.0
    return jnp.asarray(np.concatenate([matrix, matrix], axis=0), jnp.bfloat16)


def halves(value):
    high = value.astype(jnp.bfloat16)
    low = (value - high.astype(jnp.float32)).astype(jnp.bfloat16)
    return high, low


def dot(a, b):
    return jnp.dot(a, b, preferred_element_type=jnp.float32)


def columns(*rows):
    have = sum(r.shape[0] for r in rows)
    pad = -have % 8
    parts = list(rows) + ([jnp.zeros((pad, C), jnp.float32)] if pad else [])
    stacked = jnp.concatenate(parts, axis=0) if len(parts) > 1 else parts[0]
    stacked = jnp.concatenate([stacked, jnp.zeros((have + pad, LANES - C), jnp.float32)], axis=1)
    return jnp.transpose(stacked)


def spread(column, lanes):
    return jnp.broadcast_to(column, (column.shape[0], lanes))


def normed(field, gain):
    meansq = jnp.sum(field * field, axis=0, keepdims=True) * (1.0 / C)
    return field * lax.rsqrt(meansq + 1e-06) * gain


def tail(count, first, field, conv, mixers, matrix, gain, parts, field_out, next_out, sent=None):
    weights = jnp.concatenate([mixers[0, 0], mixers[0, 1]], axis=0) * 0.5
    weights_high, weights_low = halves(weights)
    weights_twice = jnp.concatenate([weights_high, weights_high], axis=1)
    for r in range(count):
        high, low = halves(conv[r])
        both = dot(weights_twice, jnp.concatenate([high, low], axis=0)) + dot(weights_low, high)
        value = both[:C]
        mixed = field[first + r] + value + value * jnp.tanh(both[C:])
        high, low = halves(mixed)
        rows = slice(r * C, (r + 1) * C)
        parts[rows, :SITES] = high
        parts[rows, SITES:] = low
    moved = dot(parts[...], matrix[...])
    for r in range(count):
        here = moved[r * C : (r + 1) * C]
        field_out[r] = here
        if sent is not None:
            sent(r)
        if next_out is not None:
            next_out[r] = normed(here, gain)


def rounds_kernel(
    first, state_in, events_in, embed_in, gains_in, taps_in, mixers_in, matrix_in, field_out, next_out, *work
):
    ext, state, events, embed, gains, taps, mixers, matrix, conv, parts, sems = work
    last = state.shape[0]
    count = last - first
    small = [
        (gains_in, gains),
        (taps_in, taps),
        (embed_in, embed),
        (events_in, events),
        (mixers_in.at[0:1], mixers),
        (matrix_in, matrix),
    ]
    rounds = range(max(0, first - HIST), last)
    copies = [pltpu.make_async_copy(a, b, sems.at[last + n]) for n, (a, b) in enumerate(small)]
    loads = {r: pltpu.make_async_copy(state_in.at[r], state.at[r], sems.at[r]) for r in rounds}
    for copy in copies[:4] + list(loads.values()) + copies[4:]:
        copy.start()
    for copy in copies[:4]:
        copy.wait()
    cols = columns(taps[...], gains[...], embed[...])[:C]
    gain_now = spread(cols[:, KT : KT + 1], SITES)
    gain_next = spread(cols[:, KT + 1 : KT + 2], SITES)
    embed_here = spread(cols[:, KT + 3 : KT + 4], SITES)
    for s in range(first, HIST):
        past = 2.0 * events[s : s + 1, :].astype(jnp.float32) - 1.0
        ext[s] = embed_here * past
    for r in rounds:
        loads[r].wait()
        ext[HIST + r] = normed(state[r], gain_now)
    for i in range(C // 8):
        rows = slice(i * 8, (i + 1) * 8)
        tap = [spread(cols[rows, k : k + 1], LANES) for k in range(KT)]
        for half in range(2):
            lanes = slice(half * LANES, (half + 1) * LANES)
            seen = [ext[first + s, rows, lanes] for s in range(count + KT - 1)]
            for r in range(count):
                total = tap[0] * seen[r]
                for k in range(1, KT):
                    total = total + tap[k] * seen[r + k]
                conv[r, rows, lanes] = total
    for copy in copies[4:]:
        copy.wait()
    tail(count, first, state, conv, mixers, matrix, gain_next, parts, field_out, next_out)


def tables_kernel(taps, own, far):
    lane_place = lax.broadcasted_iota(jnp.int32, (8, LANES), 1) // 8
    cols = columns(taps[...])[:C]
    for i in range(C // 8):
        rows = slice(i * 8, (i + 1) * 8)
        tap = [spread(cols[rows, k : k + 1], LANES) for k in range(2 * HALF + 1)]
        for d in range(HALF):
            keep = turned_place(lane_place, d) >= d
            own[d, rows, :] = jnp.where(keep, tap[d + HALF], tap[d])
            far[d, rows, :] = jnp.where(keep, tap[d], tap[d + HALF])
        far[HALF, rows, :] = tap[2 * HALF]


def turned_place(lane_place, d):
    return lax.rem(lane_place + 1, HALF) if d % 2 else lane_place


def lattice_kernel(axis, ends, part, *refs):
    field, own, odd, even, gains, tap_own, tap_far, mixers, matrix = refs[:9]
    if ends:
        result, conv, parts, sems = refs[-4:]
    else:
        field_out, next_out, conv, parts = refs[9:]
        gain = spread(columns(gains[...])[:C, 2:3], SITES)
    count = field.shape[0]
    lane_place = lax.broadcasted_iota(jnp.int32, (8, LANES), 1) // 8
    first_of_pair = lax.rem(lax.axis_index(axis), 2) == 0

    def conv_tile(i, carry):
        rows = pl.ds(pl.multiple_of(i * 8, 8), 8)
        for r0 in range(0, count, 2):
            spots = [
                (r, slice(half * LANES, (half + 1) * LANES)) for r in range(r0, r0 + 2) for half in range(2)
            ]
            here = [own[r, rows, lanes] for r, lanes in spots]
            one = [even[r, rows, lanes] for r, lanes in spots]
            two = [odd[r, rows, lanes] for r, lanes in spots]
            low = [jnp.where(first_of_pair, b, a) for a, b in zip(one, two)]
            high = [jnp.where(first_of_pair, a, b) for a, b in zip(one, two)]
            turned = [[pltpu.roll(v, LANES - 8, 1) for v in vs] for vs in (here, low, high)]
            sides = ((here, low, high), turned)
            totals = [tap_far[HALF, rows, :] * high[n] for n in range(len(spots))]
            for d in range(0, HALF, 2):
                sums = [None] * len(spots)
                for e in (d, d + 1):
                    near = tap_own[e, rows, :]
                    far = tap_far[e, rows, :]
                    keep = turned_place(lane_place, e) >= e
                    mine, under, over = sides[e - d]
                    for n in range(len(spots)):
                        other = jnp.where(keep, under[n], over[n]) if e else under[n]
                        piece = near * mine[n] + far * other
                        sums[n] = piece if e == d else sums[n] + piece
                for n in range(len(spots)):
                    totals[n] = totals[n] + (pltpu.roll(sums[n], LANES - 8 * d, 1) if d else sums[n])
            for n, (r, lanes) in enumerate(spots):
                conv[r, rows, lanes] = totals[n]
        return carry

    lax.fori_loop(0, C // 8, conv_tile, 0)
    if not ends:
        tail(count, 0, field, conv, mixers, matrix, gain, parts, field_out, next_out)
        return

    copies = [
        pltpu.make_async_copy(conv.at[r], result.at[part * CHUNK + r], sems.at[r]) for r in range(count)
    ]
    tail(count, 0, field, conv, mixers, matrix, None, parts, conv, None, lambda r: copies[r].start())
    for copy in copies:
        copy.wait()


def whole(shape):
    return pl.BlockSpec(shape, lambda *_: (0,) * len(shape))


def picked(shape, place):
    return pl.BlockSpec((1,) + shape[1:], lambda *_: (place,) + (0,) * (len(shape) - 1))


def cost(flops):
    return pl.CostEstimate(flops=flops, bytes_accessed=100_000, transcendentals=0)


PARAMS = pltpu.CompilerParams(vmem_limit_bytes=VMEM)
BLOCK = (CHUNK, C, SITES)
FULL = (ROUNDS, C, SITES)
WORK = [pltpu.VMEM(BLOCK, jnp.float32), pltpu.VMEM((CHUNK * C, 2 * SITES), jnp.bfloat16)]


def rounds_pass(part, inputs):
    state, events, embed, gains, taps, mixers, matrix = inputs
    first = part * CHUNK
    last = first + CHUNK
    outs = [BLOCK, BLOCK]
    return pl.pallas_call(
        functools.partial(rounds_kernel, first),
        grid=(1,),
        in_specs=[pl.BlockSpec(memory_space=pltpu.HBM)] * 7,
        out_specs=[whole(o) for o in outs],
        out_shape=[jax.ShapeDtypeStruct(o, jnp.float32) for o in outs],
        scratch_shapes=[
            pltpu.VMEM((HIST + last, C, SITES), jnp.float32),
            pltpu.VMEM((last, C, SITES), jnp.float32),
            pltpu.VMEM(events.shape, jnp.int32),
            pltpu.VMEM(embed.shape, jnp.float32),
            pltpu.VMEM(gains.shape, jnp.float32),
            pltpu.VMEM(taps.shape, jnp.float32),
            pltpu.VMEM((1,) + mixers.shape[1:], jnp.float32),
            pltpu.VMEM(matrix.shape, jnp.bfloat16),
        ]
        + WORK
        + [pltpu.SemaphoreType.DMA((last + 6,))],
        compiler_params=PARAMS,
        cost_estimate=cost(20_000_000),
    )(*inputs)


def tap_tables(taps):
    outs = [jax.ShapeDtypeStruct((HALF + n, C, LANES), jnp.float32) for n in range(2)]
    return pl.pallas_call(
        tables_kernel,
        grid=(1,),
        in_specs=[whole(taps.shape)],
        out_specs=[whole(o.shape) for o in outs],
        out_shape=outs,
        compiler_params=PARAMS,
        cost_estimate=cost(1_000_000),
    )(taps)


def lattice_pass(axis, field, own, sides, gains, table, mixers, matrix):
    args = (field, own, *sides, gains, *table, mixers, matrix)
    return pl.pallas_call(
        functools.partial(lattice_kernel, axis, False, 0),
        grid=(1,),
        in_specs=[whole(a.shape) for a in args[:-2]] + [picked(mixers.shape, 1), whole(matrix.shape)],
        out_specs=[whole(BLOCK)] * 2,
        out_shape=[jax.ShapeDtypeStruct(BLOCK, jnp.float32)] * 2,
        scratch_shapes=WORK,
        compiler_params=PARAMS,
        cost_estimate=cost(1_200_000_000),
    )(*args)


def last_pass(axis, part, result, field, own, sides, gains, table, mixers, matrix):
    args = (field, own, *sides, gains, *table, mixers, matrix)
    specs = [whole(a.shape) for a in args[:-2]] + [picked(mixers.shape, 2), whole(matrix.shape)]
    aliases = {}
    if result is not None:
        aliases = {len(args): 0}
        args = args + (result,)
        specs = specs + [pl.BlockSpec(memory_space=pl.ANY)]
    return pl.pallas_call(
        functools.partial(lattice_kernel, axis, True, part),
        grid=(1,),
        in_specs=specs,
        out_specs=pl.BlockSpec(memory_space=pl.ANY),
        out_shape=jax.ShapeDtypeStruct(FULL, jnp.float32),
        scratch_shapes=WORK + [pltpu.SemaphoreType.DMA((CHUNK,))],
        input_output_aliases=aliases,
        compiler_params=PARAMS,
        cost_estimate=cost(1_200_000_000),
    )(*args)


def swap(own, axis, start):
    count = lax.axis_size(axis)
    pairs = [p for i in range(start, count - 1, 2) for p in ((i, i + 1), (i + 1, i))]
    return lax.ppermute(own, axis, pairs)


def local(state, events, event_embed, gains, taps_t, taps_y, taps_x, mixers):
    native, along_y, along_x = lane_orders()
    to_y = moving(native, along_y)
    to_x = moving(along_y, along_x)
    back = moving(along_x, native)
    inputs = [
        pltpu.with_memory_space_constraint(a, pltpu.HBM)
        for a in (state, events, event_embed[None, :], gains, taps_t.T, mixers, to_y)
    ]

    field_a, own_a = rounds_pass(0, inputs)
    odd_a = swap(own_a, "gy", 1)
    even_a = swap(own_a, "gy", 0)
    field_b, own_b = rounds_pass(1, inputs)
    even_b = swap(own_b, "gy", 0)
    taps_y, own_b = lax.optimization_barrier((taps_y, own_b))
    table_y = tap_tables(taps_y.T)
    own_b, table_y = lax.optimization_barrier((own_b, table_y))
    odd_b = swap(own_b, "gy", 1)
    field_a, own_a = lattice_pass("gy", field_a, own_a, (odd_a, even_a), gains, table_y, mixers, to_x)
    even_a = swap(own_a, "gx", 0)
    odd_a = swap(own_a, "gx", 1)
    field_b, own_b = lattice_pass("gy", field_b, own_b, (odd_b, even_b), gains, table_y, mixers, to_x)
    even_b = swap(own_b, "gx", 0)
    odd_b = swap(own_b, "gx", 1)
    taps_x, own_b = lax.optimization_barrier((taps_x, own_b))
    table_x = tap_tables(taps_x.T)
    result = last_pass("gx", 0, None, field_a, own_a, (odd_a, even_a), gains, table_x, mixers, back)
    return last_pass("gx", 1, result, field_b, own_b, (odd_b, even_b), gains, table_x, mixers, back)


def solution(mesh):
    placed = (P(None, None, ("gx", "gy")), P(None, ("gx", "gy")), P(), P(), P(), P(), P(), P())
    return jax.shard_map(
        local, mesh=mesh, in_specs=placed, out_specs=P(None, None, ("gx", "gy")), check_vma=False
    )
```

time: 133 us -> 62.2 us (0.47)
  the two profiles are of different devices: /device:TPU:238 before, /device:TPU:280 now
where the time goes in v1:
time: 62.2 us; the launch traced here: 61.8 us
  starting transfers between devices  25.2 us (41%)
  Pallas kernels  22.8 us (37%)
  waiting for transfers between devices  13.6 us (22%)
    ppermute x8, starting transfers between devices, swap(): return lax.ppermute(own, axis, pairs)  25.2 us
    ppermute x8, waiting for transfers between devices, swap(): return lax.ppermute(own, axis, pairs)  13.6 us
    pallas_call x2, Pallas kernels, last_pass(): pl.pallas_call(functools.partial(lattice_kernel, axis, True, part), grid=...  8.55 us
    pallas_call x2, Pallas kernels, lattice_pass(): pl.pallas_call(functools.partial(lattice_kernel, axis, False, 0), grid=(1...  7.47 us
    pallas_call x2, Pallas kernels, rounds_pass(): pl.pallas_call(functools.partial(rounds_kernel, first), grid=(1,), in_spe...  5.12 us
    pallas_call x2, Pallas kernels, tap_tables(): pl.pallas_call(tables_kernel, grid=(1,), in_specs=[whole(taps.shape)], ou...  1.68 us
  transfers between devices with their start and end apart: 8, of which 3 were waited for; matrix products, arithmetic and copies ran while one was open for 0% of the time, Pallas kernels for 26%

profile of v1, /device:TPU:280, one launch (start us, length us, event | category | flops | bytes accessed | tf_op | source)
XLA Modules:
  0.0 61.8 jit_solution(2279514897757188730)
XLA Ops:
  0.0 2.4 %shard_map.113 = (f32[6,96,256]{2,1,0:T(8,128)S(1)}, f32[6,96,256]{2,1,0:T(8,128)S(1)}) custom-call(f32[12,96,256]{2,1,0:T(8,128)} %state_in.3, s32[8,256]{1,0:T(8,128)} %events_in.3, f32[1,96]{1,0:T(1,128)} %bitcast.8, f32[3,96]{1,0:T(4,128)} %refs_4_.7, f32[9,96]{1,0:T(8,128)} %bitcast.6, f32[3,2,96,96]{3,2,1,0:T(8,128)} %refs_7_.7, ...), custom_call_target="tpu_custom_call" | custom-call | flops 20000000 | bytes 100000 | tf_op jit(solution)/shard_map/pallas_call | solution.py:229
  2.4 0.0 copy-start.4
  2.4 0.0 copy-start
  2.4 0.0 copy-start.1
  2.5 0.0 copy-start.3
  2.5 2.1 %collective-permute-start.5 = (f32[6,96,256]{2,1,0:T(8,128)S(1)}, f32[6,96,256]{2,1,0:T(8,128)S(1)}, u32[]{:S(2)}, u32[]{:S(2)}) collective-permute-start(f32[6,96,256]{2,1,0:T(8,128)S(1)} %get-tuple-element.40.refs_1_), channel_id=1, source_target_pairs={{0,1},{1,0},{2,3},{3,2},{4,5},{5,4},{6,7},{7,6},{8,9},{9,8},{10,11... | collective-permute-start | bytes 1769480 | tf_op jit(solution)/shard_map/ppermute | solution.py:303
  4.5 2.5 %collective-permute-start.4 = (f32[6,96,256]{2,1,0:T(8,128)S(1)}, f32[6,96,256]{2,1,0:T(8,128)S(1)}, u32[]{:S(2)}, u32[]{:S(2)}) collective-permute-start(f32[6,96,256]{2,1,0:T(8,128)S(1)} %get-tuple-element.40.refs_1_), channel_id=1, source_target_pairs={{1,2},{2,1},{3,4},{4,3},{5,6},{6,5},{7,8},{8,7},{9,10},{10,9},{11,... | collective-permute-start | bytes 1769480 | tf_op jit(solution)/shard_map/ppermute | solution.py:303
  7.0 2.7 %shard_map.109 = (f32[6,96,256]{2,1,0:T(8,128)S(1)}, f32[6,96,256]{2,1,0:T(8,128)S(1)}) custom-call(f32[12,96,256]{2,1,0:T(8,128)} %state_in.3, s32[8,256]{1,0:T(8,128)} %events_in.3, f32[1,96]{1,0:T(1,128)} %bitcast.9, f32[3,96]{1,0:T(4,128)} %refs_4_.7, f32[9,96]{1,0:T(8,128)} %bitcast.7, f32[3,2,96,96]{3,2,1,0:T(8,128)} %refs_7_.7, ...), custom_call_target="tpu_custom_call" | custom-call | flops 20000000 | bytes 100000 | tf_op jit(solution)/shard_map/pallas_call | solution.py:229
  9.7 4.3 %collective-permute-start.1 = (f32[6,96,256]{2,1,0:T(8,128)S(1)}, f32[6,96,256]{2,1,0:T(8,128)S(1)}, u32[]{:S(2)}, u32[]{:S(2)}) collective-permute-start(f32[6,96,256]{2,1,0:T(8,128)S(1)} %get-tuple-element.30.refs_1_), channel_id=1, source_target_pairs={{0,1},{1,0},{2,3},{3,2},{4,5},{5,4},{6,7},{7,6},{8,9},{9,8},{10,11... | collective-permute-start | bytes 1769480 | tf_op jit(solution)/shard_map/ppermute | solution.py:303
  14.0 0.8 %shard_map.110 = (f32[16,96,128]{2,1,0:T(8,128)S(1)}, f32[17,96,128]{2,1,0:T(8,128)S(1)}) custom-call(f32[33,96]{1,0:T(8,128)S(1)} %bitcast.4), custom_call_target="tpu_custom_call" | custom-call | flops 1000000 | bytes 100000 | tf_op jit(solution)/shard_map/pallas_call | solution.py:254
  14.9 1.9 %collective-permute-start = (f32[6,96,256]{2,1,0:T(8,128)S(1)}, f32[6,96,256]{2,1,0:T(8,128)S(1)}, u32[]{:S(2)}, u32[]{:S(2)}) collective-permute-start(f32[6,96,256]{2,1,0:T(8,128)S(1)} %get-tuple-element.30.refs_1_), channel_id=1, source_target_pairs={{1,2},{2,1},{3,4},{4,3},{5,6},{6,5},{7,8},{8,7},{9,10},{10,9},{11,... | collective-permute-start | bytes 1769480 | tf_op jit(solution)/shard_map/ppermute | solution.py:303
  16.8 3.7 %shard_map.114 = (f32[6,96,256]{2,1,0:T(8,128)S(1)}, f32[6,96,256]{2,1,0:T(8,128)S(1)}) custom-call(f32[6,96,256]{2,1,0:T(8,128)S(1)} %get-tuple-element.39.refs_0_, f32[6,96,256]{2,1,0:T(8,128)S(1)} %get-tuple-element.40.refs_1_, f32[6,96,256]{2,1,0:T(8,128)S(1)} %collective-permute-done.4.refs_2_, f32[6,96,256]{2,1,0:T(8,128)S(1)} %collective-permute-done.5.refs_3_, ...), custom_call_target="tpu_custom_call" | custom-call | flops 1200000000 | bytes 100000 | tf_op jit(solution)/shard_map/pallas_call | solution.py:267
  20.6 3.4 %collective-permute-start.7 = (f32[6,96,256]{2,1,0:T(8,128)S(1)}, f32[6,96,256]{2,1,0:T(8,128)S(1)}, u32[]{:S(2)}, u32[]{:S(2)}) collective-permute-start(f32[6,96,256]{2,1,0:T(8,128)S(1)} %get-tuple-element.42.refs_1_), channel_id=1, source_target_pairs={{0,16},{16,0},{32,48},{48,32},{64,80},{80,64},{96,112},{112,96},{1... | collective-permute-start | bytes 1769480 | tf_op jit(solution)/shard_map/ppermute | solution.py:303
  24.0 3.1 %collective-permute-start.6 = (f32[6,96,256]{2,1,0:T(8,128)S(1)}, f32[6,96,256]{2,1,0:T(8,128)S(1)}, u32[]{:S(2)}, u32[]{:S(2)}) collective-permute-start(f32[6,96,256]{2,1,0:T(8,128)S(1)} %get-tuple-element.42.refs_1_), channel_id=1, source_target_pairs={{16,32},{32,16},{48,64},{64,48},{80,96},{96,80},{112,128},{128,112... | collective-permute-start | bytes 1769480 | tf_op jit(solution)/shard_map/ppermute | solution.py:303
  27.1 0.0 copy-start.2
  27.1 3.7 %shard_map.111 = (f32[6,96,256]{2,1,0:T(8,128)S(1)}, f32[6,96,256]{2,1,0:T(8,128)S(1)}) custom-call(f32[6,96,256]{2,1,0:T(8,128)S(1)} %get-tuple-element.24.refs_0_, f32[6,96,256]{2,1,0:T(8,128)S(1)} %get-tuple-element.30.refs_1_, f32[6,96,256]{2,1,0:T(8,128)S(1)} %collective-permute-done.refs_2_, f32[6,96,256]{2,1,0:T(8,128)S(1)} %collective-permute-done.1.refs_3_, ...), custom_call_target="tpu_custom_call" | custom-call | flops 1200000000 | bytes 100000 | tf_op jit(solution)/shard_map/pallas_call | solution.py:267
  30.9 3.4 %collective-permute-start.3 = (f32[6,96,256]{2,1,0:T(8,128)S(1)}, f32[6,96,256]{2,1,0:T(8,128)S(1)}, u32[]{:S(2)}, u32[]{:S(2)}) collective-permute-start(f32[6,96,256]{2,1,0:T(8,128)S(1)} %get-tuple-element.35.refs_1_), channel_id=1, source_target_pairs={{0,16},{16,0},{32,48},{48,32},{64,80},{80,64},{96,112},{112,96},{1... | collective-permute-start | bytes 1769480 | tf_op jit(solution)/shard_map/ppermute | solution.py:303
  34.3 4.6 %collective-permute-start.2 = (f32[6,96,256]{2,1,0:T(8,128)S(1)}, f32[6,96,256]{2,1,0:T(8,128)S(1)}, u32[]{:S(2)}, u32[]{:S(2)}) collective-permute-start(f32[6,96,256]{2,1,0:T(8,128)S(1)} %get-tuple-element.35.refs_1_), channel_id=1, source_target_pairs={{16,32},{32,16},{48,64},{64,48},{80,96},{96,80},{112,128},{128,112... | collective-permute-start | bytes 1769480 | tf_op jit(solution)/shard_map/ppermute | solution.py:303
  38.9 0.8 %shard_map.112 = (f32[16,96,128]{2,1,0:T(8,128)S(1)}, f32[17,96,128]{2,1,0:T(8,128)S(1)}) custom-call(f32[33,96]{1,0:T(8,128)S(1)} %bitcast.5), custom_call_target="tpu_custom_call" | custom-call | flops 1000000 | bytes 100000 | tf_op jit(solution)/shard_map/pallas_call | solution.py:254
  39.7 5.6 %collective-permute-done.6.refs_2_ = f32[6,96,256]{2,1,0:T(8,128)S(1)} collective-permute-done((f32[6,96,256]{2,1,0:T(8,128)S(1)}, f32[6,96,256]{2,1,0:T(8,128)S(1)}, u32[]{:S(2)}, u32[]{:S(2)}) %collective-permute-start.6) | collective-permute-done | bytes 589856 | tf_op jit(solution)/shard_map/ppermute | solution.py:303
  45.3 4.3 %shard_map.115.refs_9_ = f32[12,96,256]{2,1,0:T(8,128)} custom-call(f32[6,96,256]{2,1,0:T(8,128)S(1)} %get-tuple-element.41.refs_0_, f32[6,96,256]{2,1,0:T(8,128)S(1)} %get-tuple-element.42.refs_1_, f32[6,96,256]{2,1,0:T(8,128)S(1)} %collective-permute-done.6.refs_2_, f32[6,96,256]{2,1,0:T(8,128)S(1)} %collective-permute-done.7.refs_3_, ...), custom_call_target="tpu_custom_call" | custom-call | flops 1200000000 | bytes 100000 | tf_op jit(solution)/shard_map/pallas_call | solution.py:287
  49.6 1.5 %collective-permute-done.3.refs_3_ = f32[6,96,256]{2,1,0:T(8,128)S(1)} collective-permute-done((f32[6,96,256]{2,1,0:T(8,128)S(1)}, f32[6,96,256]{2,1,0:T(8,128)S(1)}, u32[]{:S(2)}, u32[]{:S(2)}) %collective-permute-start.3) | collective-permute-done | bytes 589856 | tf_op jit(solution)/shard_map/ppermute | solution.py:303
  51.1 6.4 %collective-permute-done.2.refs_2_ = f32[6,96,256]{2,1,0:T(8,128)S(1)} collective-permute-done((f32[6,96,256]{2,1,0:T(8,128)S(1)}, f32[6,96,256]{2,1,0:T(8,128)S(1)}, u32[]{:S(2)}, u32[]{:S(2)}) %collective-permute-start.2) | collective-permute-done | bytes 589856 | tf_op jit(solution)/shard_map/ppermute | solution.py:303
  57.6 4.3 %shard_map.116 = f32[12,96,256]{2,1,0:T(8,128)} custom-call(f32[6,96,256]{2,1,0:T(8,128)S(1)} %get-tuple-element.33.refs_0_, f32[6,96,256]{2,1,0:T(8,128)S(1)} %get-tuple-element.35.refs_1_, f32[6,96,256]{2,1,0:T(8,128)S(1)} %collective-permute-done.2.refs_2_, f32[6,96,256]{2,1,0:T(8,128)S(1)} %collective-permute-done.3.refs_3_, ...), custom_call_target="tpu_custom_call", output_to_operand_aliasing={{}: (9, {})} | custom-call | flops 1200000000 | bytes 100000 | tf_op jit(solution)/shard_map/pallas_call | solution.py:287
  (12 shorter events, 0.0 us)
Async XLA Ops:
  2.4 11.6 %copy-start.4 = (f32[96,33]{0,1:T(8,128)S(1)}, f32[96,33]{0,1:T(8,128)}, u32[]{:S(2)}) copy-start(f32[96,33]{0,1:T(8,128)} %param.16) | copy-start | bytes 38020
  2.4 14.4 %copy-start = (f32[3,2,96,96]{3,2,1,0:T(8,128)S(1)}, f32[3,2,96,96]{3,2,1,0:T(8,128)}, u32[]{:S(2)}) copy-start(f32[3,2,96,96]{3,2,1,0:T(8,128)} %refs_7_.7) | copy-start | bytes 663556
  2.4 14.4 %copy-start.1 = (bf16[512,256]{1,0:T(8,128)(2,1)S(1)}, bf16[512,256]{1,0:T(8,128)(2,1)}, u32[]{:S(2)}) copy-start(bf16[512,256]{1,0:T(8,128)(2,1)} %constant.7.clone.refs_8_) | copy-start | bytes 786436
  2.5 14.4 %copy-start.3 = (f32[3,96]{1,0:T(4,128)S(1)}, f32[3,96]{1,0:T(4,128)}, u32[]{:S(2)}) copy-start(f32[3,96]{1,0:T(4,128)} %refs_4_.7) | copy-start | bytes 3460
  2.5 14.3 %collective-permute-start.5 = (f32[6,96,256]{2,1,0:T(8,128)S(1)}, f32[6,96,256]{2,1,0:T(8,128)S(1)}, u32[]{:S(2)}, u32[]{:S(2)}) collective-permute-start(f32[6,96,256]{2,1,0:T(8,128)S(1)} %get-tuple-element.40.refs_1_), channel_id=1, source_target_pairs={{0,1},{1,0},{2,3},{3,2},{4,5},{5,4},{6,7},{7,6},{8,9},{9,8},{10,11... | collective-permute-start | bytes 1769480 | tf_op jit(solution)/shard_map/ppermute | solution.py:303
  4.5 12.3 %collective-permute-start.4 = (f32[6,96,256]{2,1,0:T(8,128)S(1)}, f32[6,96,256]{2,1,0:T(8,128)S(1)}, u32[]{:S(2)}, u32[]{:S(2)}) collective-permute-start(f32[6,96,256]{2,1,0:T(8,128)S(1)} %get-tuple-element.40.refs_1_), channel_id=1, source_target_pairs={{1,2},{2,1},{3,4},{4,3},{5,6},{6,5},{7,8},{8,7},{9,10},{10,9},{11,... | collective-permute-start | bytes 1769480 | tf_op jit(solution)/shard_map/ppermute | solution.py:303
  9.7 17.4 %collective-permute-start.1 = (f32[6,96,256]{2,1,0:T(8,128)S(1)}, f32[6,96,256]{2,1,0:T(8,128)S(1)}, u32[]{:S(2)}, u32[]{:S(2)}) collective-permute-start(f32[6,96,256]{2,1,0:T(8,128)S(1)} %get-tuple-element.30.refs_1_), channel_id=1, source_target_pairs={{0,1},{1,0},{2,3},{3,2},{4,5},{5,4},{6,7},{7,6},{8,9},{9,8},{10,11... | collective-permute-start | bytes 1769480 | tf_op jit(solution)/shard_map/ppermute | solution.py:303
  14.9 12.2 %collective-permute-start = (f32[6,96,256]{2,1,0:T(8,128)S(1)}, f32[6,96,256]{2,1,0:T(8,128)S(1)}, u32[]{:S(2)}, u32[]{:S(2)}) collective-permute-start(f32[6,96,256]{2,1,0:T(8,128)S(1)} %get-tuple-element.30.refs_1_), channel_id=1, source_target_pairs={{1,2},{2,1},{3,4},{4,3},{5,6},{6,5},{7,8},{8,7},{9,10},{10,9},{11,... | collective-permute-start | bytes 1769480 | tf_op jit(solution)/shard_map/ppermute | solution.py:303
  20.6 19.1 %collective-permute-start.7 = (f32[6,96,256]{2,1,0:T(8,128)S(1)}, f32[6,96,256]{2,1,0:T(8,128)S(1)}, u32[]{:S(2)}, u32[]{:S(2)}) collective-permute-start(f32[6,96,256]{2,1,0:T(8,128)S(1)} %get-tuple-element.42.refs_1_), channel_id=1, source_target_pairs={{0,16},{16,0},{32,48},{48,32},{64,80},{80,64},{96,112},{112,96},{1... | collective-permute-start | bytes 1769480 | tf_op jit(solution)/shard_map/ppermute | solution.py:303
  24.0 21.3 %collective-permute-start.6 = (f32[6,96,256]{2,1,0:T(8,128)S(1)}, f32[6,96,256]{2,1,0:T(8,128)S(1)}, u32[]{:S(2)}, u32[]{:S(2)}) collective-permute-start(f32[6,96,256]{2,1,0:T(8,128)S(1)} %get-tuple-element.42.refs_1_), channel_id=1, source_target_pairs={{16,32},{32,16},{48,64},{64,48},{80,96},{96,80},{112,128},{128,112... | collective-permute-start | bytes 1769480 | tf_op jit(solution)/shard_map/ppermute | solution.py:303
  27.1 11.8 %copy-start.5 = (f32[96,33]{0,1:T(8,128)S(1)}, f32[96,33]{0,1:T(8,128)}, u32[]{:S(2)}) copy-start(f32[96,33]{0,1:T(8,128)} %param.17) | copy-start | bytes 38020
  27.1 18.2 %copy-start.2 = (bf16[512,256]{1,0:T(8,128)(2,1)S(1)}, bf16[512,256]{1,0:T(8,128)(2,1)}, u32[]{:S(2)}) copy-start(bf16[512,256]{1,0:T(8,128)(2,1)} %constant.8.clone.refs_8_) | copy-start | bytes 786436
  30.9 20.3 %collective-permute-start.3 = (f32[6,96,256]{2,1,0:T(8,128)S(1)}, f32[6,96,256]{2,1,0:T(8,128)S(1)}, u32[]{:S(2)}, u32[]{:S(2)}) collective-permute-start(f32[6,96,256]{2,1,0:T(8,128)S(1)} %get-tuple-element.35.refs_1_), channel_id=1, source_target_pairs={{0,16},{16,0},{32,48},{48,32},{64,80},{80,64},{96,112},{112,96},{1... | collective-permute-start | bytes 1769480 | tf_op jit(solution)/shard_map/ppermute | solution.py:303
  34.3 23.3 %collective-permute-start.2 = (f32[6,96,256]{2,1,0:T(8,128)S(1)}, f32[6,96,256]{2,1,0:T(8,128)S(1)}, u32[]{:S(2)}, u32[]{:S(2)}) collective-permute-start(f32[6,96,256]{2,1,0:T(8,128)S(1)} %get-tuple-element.35.refs_1_), channel_id=1, source_target_pairs={{16,32},{32,16},{48,64},{64,48},{80,96},{96,80},{112,128},{128,112... | collective-permute-start | bytes 1769480 | tf_op jit(solution)/shard_map/ppermute | solution.py:303

commit v2 on v1

--- a/solution.py
+++ b/solution.py
@@ -131,21 +131,25 @@
     tail(count, first, state, conv, mixers, matrix, gain_next, parts, field_out, next_out)
 
 
-def tables_kernel(taps, own, far):
+def tables_kernel(kinds, taps, *tables):
     lane_place = lax.broadcasted_iota(jnp.int32, (8, LANES), 1) // 8
     cols = columns(taps[...])[:C]
     for i in range(C // 8):
         rows = slice(i * 8, (i + 1) * 8)
         tap = [spread(cols[rows, k : k + 1], LANES) for k in range(2 * HALF + 1)]
-        for d in range(HALF):
-            keep = turned_place(lane_place, d) >= d
-            own[d, rows, :] = jnp.where(keep, tap[d + HALF], tap[d])
-            far[d, rows, :] = jnp.where(keep, tap[d], tap[d + HALF])
-        far[HALF, rows, :] = tap[2 * HALF]
+        for kind, table in zip(kinds, tables):
+            for d in range(HALF):
+                keep = turned_place(lane_place, d) >= d
+                if kind == "own":
+                    table[d, rows, :] = jnp.where(keep, tap[d + HALF], tap[d])
+                else:
+                    table[d, rows, :] = jnp.where(keep, tap[d], tap[d + HALF])
+            if kind == "far":
+                table[HALF, rows, :] = tap[2 * HALF]
 
 
 def turned_place(lane_place, d):
-    return lax.rem(lane_place + 1, HALF) if d % 2 else lane_place
+    return (lane_place + 1) & (HALF - 1) if d % 2 else lane_place
 
 
 def lattice_kernel(axis, ends, part, *refs):
@@ -249,17 +253,18 @@
     )(*inputs)
 
 
-def tap_tables(taps):
-    outs = [jax.ShapeDtypeStruct((HALF + n, C, LANES), jnp.float32) for n in range(2)]
+def tap_tables(kinds, taps, after):
+    taps, after = lax.optimization_barrier((taps, after))
+    outs = [jax.ShapeDtypeStruct((HALF + (kind == "far"), C, LANES), jnp.float32) for kind in kinds]
     return pl.pallas_call(
-        tables_kernel,
+        functools.partial(tables_kernel, kinds),
         grid=(1,),
-        in_specs=[whole(taps.shape)],
+        in_specs=[whole(taps.shape[::-1])],
         out_specs=[whole(o.shape) for o in outs],
         out_shape=outs,
         compiler_params=PARAMS,
         cost_estimate=cost(1_000_000),
-    )(taps)
+    )(taps.T)
 
 
 def lattice_pass(axis, field, own, sides, gains, table, mixers, matrix):
@@ -315,21 +320,20 @@
 
     field_a, own_a = rounds_pass(0, inputs)
     odd_a = swap(own_a, "gy", 1)
-    even_a = swap(own_a, "gy", 0)
+    table_y, held = lax.optimization_barrier((tap_tables(("own", "far"), taps_y, own_a), own_a))
+    even_a = swap(held, "gy", 0)
     field_b, own_b = rounds_pass(1, inputs)
+    odd_b = swap(own_b, "gy", 1)
     even_b = swap(own_b, "gy", 0)
-    taps_y, own_b = lax.optimization_barrier((taps_y, own_b))
-    table_y = tap_tables(taps_y.T)
-    own_b, table_y = lax.optimization_barrier((own_b, table_y))
-    odd_b = swap(own_b, "gy", 1)
     field_a, own_a = lattice_pass("gy", field_a, own_a, (odd_a, even_a), gains, table_y, mixers, to_x)
-    even_a = swap(own_a, "gx", 0)
     odd_a = swap(own_a, "gx", 1)
+    near_x, held = lax.optimization_barrier((tap_tables(("own",), taps_x, own_a), own_a))
+    even_a = swap(held, "gx", 0)
     field_b, own_b = lattice_pass("gy", field_b, own_b, (odd_b, even_b), gains, table_y, mixers, to_x)
-    even_b = swap(own_b, "gx", 0)
     odd_b = swap(own_b, "gx", 1)
-    taps_x, own_b = lax.optimization_barrier((taps_x, own_b))
-    table_x = tap_tables(taps_x.T)
+    far_x, held = lax.optimization_barrier((tap_tables(("far",), taps_x, own_b), own_b))
+    even_b = swap(held, "gx", 0)
+    table_x = (*near_x, *far_x)
     result = last_pass("gx", 0, None, field_a, own_a, (odd_a, even_a), gains, table_x, mixers, back)
     return last_pass("gx", 1, result, field_b, own_b, (odd_b, even_b), gains, table_x, mixers, back)
 

time: 62.2 us -> 61.7 us (level)
  the two profiles are of different devices: /device:TPU:280 before, /device:TPU:222 now
where the time goes in v2:
time: 61.7 us; the launch traced here: 61.4 us
  starting transfers between devices  24.8 us (40%)
  Pallas kernels  23.7 us (38%)
  waiting for transfers between devices  12.6 us (20%)
    ppermute x8, starting transfers between devices, swap(): return lax.ppermute(own, axis, pairs)  24.8 us
    ppermute x8, waiting for transfers between devices, swap(): return lax.ppermute(own, axis, pairs)  12.6 us
    pallas_call x2, Pallas kernels, last_pass(): pl.pallas_call(functools.partial(lattice_kernel, axis, True, part), grid=...  8.58 us
    pallas_call x2, Pallas kernels, lattice_pass(): pl.pallas_call(functools.partial(lattice_kernel, axis, False, 0), grid=(1...  7.52 us
    pallas_call x2, Pallas kernels, rounds_pass(): pl.pallas_call(functools.partial(rounds_kernel, first), grid=(1,), in_spe...  5.13 us
    pallas_call x3, Pallas kernels, tap_tables(): pl.pallas_call(functools.partial(tables_kernel, kinds), grid=(1,), in_spe...  2.49 us
  transfers between devices with their start and end apart: 8, of which 4 were waited for; matrix products, arithmetic and copies ran while one was open for 0% of the time, Pallas kernels for 28%

profile of v2, /device:TPU:222, one launch (start us, length us, event | category | flops | bytes accessed | tf_op | source)
XLA Modules:
  0.0 61.4 jit_solution(13789087917267556640)
XLA Ops:
  0.0 2.4 %shard_map.110 = (f32[6,96,256]{2,1,0:T(8,128)S(1)}, f32[6,96,256]{2,1,0:T(8,128)S(1)}) custom-call(f32[12,96,256]{2,1,0:T(8,128)} %state_in.3, s32[8,256]{1,0:T(8,128)} %events_in.3, f32[1,96]{1,0:T(1,128)} %bitcast.10, f32[3,96]{1,0:T(4,128)} %refs_4_.7, f32[9,96]{1,0:T(8,128)} %bitcast.8, f32[3,2,96,96]{3,2,1,0:T(8,128)} %refs_7_.7, ...), custom_call_target="tpu_custom_call" | custom-call | flops 20000000 | bytes 100000 | tf_op jit(solution)/shard_map/pallas_call | solution.py:233
  2.4 0.0 copy-start
  2.4 0.0 copy-start.1
  2.5 2.1 %collective-permute-start.4 = (f32[6,96,256]{2,1,0:T(8,128)S(1)}, f32[6,96,256]{2,1,0:T(8,128)S(1)}, u32[]{:S(2)}, u32[]{:S(2)}) collective-permute-start(f32[6,96,256]{2,1,0:T(8,128)S(1)} %get-tuple-element.38.refs_1_), channel_id=1, source_target_pairs={{1,2},{2,1},{3,4},{4,3},{5,6},{6,5},{7,8},{8,7},{9,10},{10,9},{11,... | collective-permute-start | bytes 1769480 | tf_op jit(solution)/shard_map/ppermute | solution.py:308
  4.5 0.8 %shard_map.111 = (f32[16,96,128]{2,1,0:T(8,128)S(1)}, f32[17,96,128]{2,1,0:T(8,128)S(1)}) custom-call(f32[33,96]{1,0:T(8,128)S(1)} %bitcast.7), custom_call_target="tpu_custom_call" | custom-call | flops 1000000 | bytes 100000 | tf_op jit(solution)/shard_map/pallas_call | solution.py:259
  5.4 4.8 %collective-permute-start.5 = (f32[6,96,256]{2,1,0:T(8,128)S(1)}, f32[6,96,256]{2,1,0:T(8,128)S(1)}, u32[]{:S(2)}, u32[]{:S(2)}) collective-permute-start(f32[6,96,256]{2,1,0:T(8,128)S(1)} %get-tuple-element.38.refs_1_), channel_id=1, source_target_pairs={{0,1},{1,0},{2,3},{3,2},{4,5},{5,4},{6,7},{7,6},{8,9},{9,8},{10,11... | collective-permute-start | bytes 1769480 | tf_op jit(solution)/shard_map/ppermute | solution.py:308
  10.2 2.7 %shard_map.109 = (f32[6,96,256]{2,1,0:T(8,128)S(1)}, f32[6,96,256]{2,1,0:T(8,128)S(1)}) custom-call(f32[12,96,256]{2,1,0:T(8,128)} %state_in.3, s32[8,256]{1,0:T(8,128)} %events_in.3, f32[1,96]{1,0:T(1,128)} %bitcast.11, f32[3,96]{1,0:T(4,128)} %refs_4_.7, f32[9,96]{1,0:T(8,128)} %bitcast.9, f32[3,2,96,96]{3,2,1,0:T(8,128)} %refs_7_.7, ...), custom_call_target="tpu_custom_call" | custom-call | flops 20000000 | bytes 100000 | tf_op jit(solution)/shard_map/pallas_call | solution.py:233
  12.9 1.9 %collective-permute-start.1 = (f32[6,96,256]{2,1,0:T(8,128)S(1)}, f32[6,96,256]{2,1,0:T(8,128)S(1)}, u32[]{:S(2)}, u32[]{:S(2)}) collective-permute-start(f32[6,96,256]{2,1,0:T(8,128)S(1)} %get-tuple-element.26.refs_1_), channel_id=1, source_target_pairs={{0,1},{1,0},{2,3},{3,2},{4,5},{5,4},{6,7},{7,6},{8,9},{9,8},{10,11... | collective-permute-start | bytes 1769480 | tf_op jit(solution)/shard_map/ppermute | solution.py:308
  14.8 1.9 %collective-permute-start = (f32[6,96,256]{2,1,0:T(8,128)S(1)}, f32[6,96,256]{2,1,0:T(8,128)S(1)}, u32[]{:S(2)}, u32[]{:S(2)}) collective-permute-start(f32[6,96,256]{2,1,0:T(8,128)S(1)} %get-tuple-element.26.refs_1_), channel_id=1, source_target_pairs={{1,2},{2,1},{3,4},{4,3},{5,6},{6,5},{7,8},{8,7},{9,10},{10,9},{11,... | collective-permute-start | bytes 1769480 | tf_op jit(solution)/shard_map/ppermute | solution.py:308
  16.8 3.8 %shard_map.114 = (f32[6,96,256]{2,1,0:T(8,128)S(1)}, f32[6,96,256]{2,1,0:T(8,128)S(1)}) custom-call(f32[6,96,256]{2,1,0:T(8,128)S(1)} %get-tuple-element.37.refs_0_, f32[6,96,256]{2,1,0:T(8,128)S(1)} %get-tuple-element.38.refs_1_, f32[6,96,256]{2,1,0:T(8,128)S(1)} %collective-permute-done.4.refs_2_, f32[6,96,256]{2,1,0:T(8,128)S(1)} %collective-permute-done.5.refs_3_, ...), custom_call_target="tpu_custom_call" | custom-call | flops 1200000000 | bytes 100000 | tf_op jit(solution)/shard_map/pallas_call | solution.py:272
  20.6 5.4 %collective-permute-start.6 = (f32[6,96,256]{2,1,0:T(8,128)S(1)}, f32[6,96,256]{2,1,0:T(8,128)S(1)}, u32[]{:S(2)}, u32[]{:S(2)}) collective-permute-start(f32[6,96,256]{2,1,0:T(8,128)S(1)} %get-tuple-element.44.refs_1_), channel_id=1, source_target_pairs={{16,32},{32,16},{48,64},{64,48},{80,96},{96,80},{112,128},{128,112... | collective-permute-start | bytes 1769480 | tf_op jit(solution)/shard_map/ppermute | solution.py:308
  26.0 0.8 %shard_map.115.refs_5_ = f32[16,96,128]{2,1,0:T(8,128)S(1)} custom-call(f32[33,96]{1,0:T(8,128)S(1)} %bitcast.5), custom_call_target="tpu_custom_call" | custom-call | flops 1000000 | bytes 100000 | tf_op jit(solution)/shard_map/pallas_call | solution.py:259
  26.8 1.9 %collective-permute-start.7 = (f32[6,96,256]{2,1,0:T(8,128)S(1)}, f32[6,96,256]{2,1,0:T(8,128)S(1)}, u32[]{:S(2)}, u32[]{:S(2)}) collective-permute-start(f32[6,96,256]{2,1,0:T(8,128)S(1)} %get-tuple-element.44.refs_1_), channel_id=1, source_target_pairs={{0,16},{16,0},{32,48},{48,32},{64,80},{80,64},{96,112},{112,96},{1... | collective-permute-start | bytes 1769480 | tf_op jit(solution)/shard_map/ppermute | solution.py:308
  28.8 0.0 copy-start.2
  28.8 3.8 %shard_map.112 = (f32[6,96,256]{2,1,0:T(8,128)S(1)}, f32[6,96,256]{2,1,0:T(8,128)S(1)}) custom-call(f32[6,96,256]{2,1,0:T(8,128)S(1)} %get-tuple-element.25.refs_0_, f32[6,96,256]{2,1,0:T(8,128)S(1)} %get-tuple-element.26.refs_1_, f32[6,96,256]{2,1,0:T(8,128)S(1)} %collective-permute-done.refs_2_, f32[6,96,256]{2,1,0:T(8,128)S(1)} %collective-permute-done.1.refs_3_, ...), custom_call_target="tpu_custom_call" | custom-call | flops 1200000000 | bytes 100000 | tf_op jit(solution)/shard_map/pallas_call | solution.py:272
  32.6 4.9 %collective-permute-start.2 = (f32[6,96,256]{2,1,0:T(8,128)S(1)}, f32[6,96,256]{2,1,0:T(8,128)S(1)}, u32[]{:S(2)}, u32[]{:S(2)}) collective-permute-start(f32[6,96,256]{2,1,0:T(8,128)S(1)} %get-tuple-element.36.refs_1_), channel_id=1, source_target_pairs={{16,32},{32,16},{48,64},{64,48},{80,96},{96,80},{112,128},{128,112... | collective-permute-start | bytes 1769480 | tf_op jit(solution)/shard_map/ppermute | solution.py:308
  37.5 0.8 %shard_map.113.refs_6_ = f32[17,96,128]{2,1,0:T(8,128)S(1)} custom-call(f32[33,96]{1,0:T(8,128)S(1)} %bitcast.6), custom_call_target="tpu_custom_call" | custom-call | flops 1000000 | bytes 100000 | tf_op jit(solution)/shard_map/pallas_call | solution.py:259
  38.3 1.9 %collective-permute-start.3 = (f32[6,96,256]{2,1,0:T(8,128)S(1)}, f32[6,96,256]{2,1,0:T(8,128)S(1)}, u32[]{:S(2)}, u32[]{:S(2)}) collective-permute-start(f32[6,96,256]{2,1,0:T(8,128)S(1)} %get-tuple-element.36.refs_1_), channel_id=1, source_target_pairs={{0,16},{16,0},{32,48},{48,32},{64,80},{80,64},{96,112},{112,96},{1... | collective-permute-start | bytes 1769480 | tf_op jit(solution)/shard_map/ppermute | solution.py:308
  40.2 1.8 %collective-permute-done.6.refs_2_ = f32[6,96,256]{2,1,0:T(8,128)S(1)} collective-permute-done((f32[6,96,256]{2,1,0:T(8,128)S(1)}, f32[6,96,256]{2,1,0:T(8,128)S(1)}, u32[]{:S(2)}, u32[]{:S(2)}) %collective-permute-start.6) | collective-permute-done | bytes 589856 | tf_op jit(solution)/shard_map/ppermute | solution.py:308
  42.0 2.8 %collective-permute-done.7.refs_3_ = f32[6,96,256]{2,1,0:T(8,128)S(1)} collective-permute-done((f32[6,96,256]{2,1,0:T(8,128)S(1)}, f32[6,96,256]{2,1,0:T(8,128)S(1)}, u32[]{:S(2)}, u32[]{:S(2)}) %collective-permute-start.7) | collective-permute-done | bytes 589856 | tf_op jit(solution)/shard_map/ppermute | solution.py:308
  44.9 4.3 %shard_map.116.refs_9_ = f32[12,96,256]{2,1,0:T(8,128)} custom-call(f32[6,96,256]{2,1,0:T(8,128)S(1)} %get-tuple-element.43.refs_0_, f32[6,96,256]{2,1,0:T(8,128)S(1)} %get-tuple-element.44.refs_1_, f32[6,96,256]{2,1,0:T(8,128)S(1)} %collective-permute-done.6.refs_2_, f32[6,96,256]{2,1,0:T(8,128)S(1)} %collective-permute-done.7.refs_3_, ...), custom_call_target="tpu_custom_call" | custom-call | flops 1200000000 | bytes 100000 | tf_op jit(solution)/shard_map/pallas_call | solution.py:292
  49.2 5.3 %collective-permute-done.2.refs_2_ = f32[6,96,256]{2,1,0:T(8,128)S(1)} collective-permute-done((f32[6,96,256]{2,1,0:T(8,128)S(1)}, f32[6,96,256]{2,1,0:T(8,128)S(1)}, u32[]{:S(2)}, u32[]{:S(2)}) %collective-permute-start.2) | collective-permute-done | bytes 589856 | tf_op jit(solution)/shard_map/ppermute | solution.py:308
  54.5 2.7 %collective-permute-done.3.refs_3_ = f32[6,96,256]{2,1,0:T(8,128)S(1)} collective-permute-done((f32[6,96,256]{2,1,0:T(8,128)S(1)}, f32[6,96,256]{2,1,0:T(8,128)S(1)}, u32[]{:S(2)}, u32[]{:S(2)}) %collective-permute-start.3) | collective-permute-done | bytes 589856 | tf_op jit(solution)/shard_map/ppermute | solution.py:308
  57.1 4.3 %shard_map.117 = f32[12,96,256]{2,1,0:T(8,128)} custom-call(f32[6,96,256]{2,1,0:T(8,128)S(1)} %get-tuple-element.33.refs_0_, f32[6,96,256]{2,1,0:T(8,128)S(1)} %get-tuple-element.36.refs_1_, f32[6,96,256]{2,1,0:T(8,128)S(1)} %collective-permute-done.2.refs_2_, f32[6,96,256]{2,1,0:T(8,128)S(1)} %collective-permute-done.3.refs_3_, ...), custom_call_target="tpu_custom_call", output_to_operand_aliasing={{}: (9, {})} | custom-call | flops 1200000000 | bytes 100000 | tf_op jit(solution)/shard_map/pallas_call | solution.py:292
  (13 shorter events, 0.0 us)
Async XLA Ops:
  0.0 4.5 %copy-start.5 = (f32[96,33]{0,1:T(8,128)S(1)}, f32[96,33]{0,1:T(8,128)}, u32[]{:S(2)}) copy-start(f32[96,33]{0,1:T(8,128)} %param.16) | copy-start | bytes 38020
  2.4 14.4 %copy-start = (f32[3,2,96,96]{3,2,1,0:T(8,128)S(1)}, f32[3,2,96,96]{3,2,1,0:T(8,128)}, u32[]{:S(2)}) copy-start(f32[3,2,96,96]{3,2,1,0:T(8,128)} %refs_7_.7) | copy-start | bytes 663556
  2.4 14.4 %copy-start.1 = (bf16[512,256]{1,0:T(8,128)(2,1)S(1)}, bf16[512,256]{1,0:T(8,128)(2,1)}, u32[]{:S(2)}) copy-start(bf16[512,256]{1,0:T(8,128)(2,1)} %constant.7.clone.refs_8_) | copy-start | bytes 786436
  2.4 14.4 %copy-start.4 = (f32[3,96]{1,0:T(4,128)S(1)}, f32[3,96]{1,0:T(4,128)}, u32[]{:S(2)}) copy-start(f32[3,96]{1,0:T(4,128)} %refs_4_.7) | copy-start | bytes 3460
  2.5 14.3 %collective-permute-start.4 = (f32[6,96,256]{2,1,0:T(8,128)S(1)}, f32[6,96,256]{2,1,0:T(8,128)S(1)}, u32[]{:S(2)}, u32[]{:S(2)}) collective-permute-start(f32[6,96,256]{2,1,0:T(8,128)S(1)} %get-tuple-element.38.refs_1_), channel_id=1, source_target_pairs={{1,2},{2,1},{3,4},{4,3},{5,6},{6,5},{7,8},{8,7},{9,10},{10,9},{11,... | collective-permute-start | bytes 1769480 | tf_op jit(solution)/shard_map/ppermute | solution.py:308
  5.4 11.4 %collective-permute-start.5 = (f32[6,96,256]{2,1,0:T(8,128)S(1)}, f32[6,96,256]{2,1,0:T(8,128)S(1)}, u32[]{:S(2)}, u32[]{:S(2)}) collective-permute-start(f32[6,96,256]{2,1,0:T(8,128)S(1)} %get-tuple-element.38.refs_1_), channel_id=1, source_target_pairs={{0,1},{1,0},{2,3},{3,2},{4,5},{5,4},{6,7},{7,6},{8,9},{9,8},{10,11... | collective-permute-start | bytes 1769480 | tf_op jit(solution)/shard_map/ppermute | solution.py:308
  12.9 15.9 %collective-permute-start.1 = (f32[6,96,256]{2,1,0:T(8,128)S(1)}, f32[6,96,256]{2,1,0:T(8,128)S(1)}, u32[]{:S(2)}, u32[]{:S(2)}) collective-permute-start(f32[6,96,256]{2,1,0:T(8,128)S(1)} %get-tuple-element.26.refs_1_), channel_id=1, source_target_pairs={{0,1},{1,0},{2,3},{3,2},{4,5},{5,4},{6,7},{7,6},{8,9},{9,8},{10,11... | collective-permute-start | bytes 1769480 | tf_op jit(solution)/shard_map/ppermute | solution.py:308
  14.8 13.9 %collective-permute-start = (f32[6,96,256]{2,1,0:T(8,128)S(1)}, f32[6,96,256]{2,1,0:T(8,128)S(1)}, u32[]{:S(2)}, u32[]{:S(2)}) collective-permute-start(f32[6,96,256]{2,1,0:T(8,128)S(1)} %get-tuple-element.26.refs_1_), channel_id=1, source_target_pairs={{1,2},{2,1},{3,4},{4,3},{5,6},{6,5},{7,8},{8,7},{9,10},{10,9},{11,... | collective-permute-start | bytes 1769480 | tf_op jit(solution)/shard_map/ppermute | solution.py:308
  16.8 9.2 %copy-start.3 = (f32[96,33]{0,1:T(8,128)S(1)}, f32[96,33]{0,1:T(8,128)}, u32[]{:S(2)}) copy-start(f32[96,33]{0,1:T(8,128)} %param.17) | copy-start | bytes 38020
  20.6 21.4 %collective-permute-start.6 = (f32[6,96,256]{2,1,0:T(8,128)S(1)}, f32[6,96,256]{2,1,0:T(8,128)S(1)}, u32[]{:S(2)}, u32[]{:S(2)}) collective-permute-start(f32[6,96,256]{2,1,0:T(8,128)S(1)} %get-tuple-element.44.refs_1_), channel_id=1, source_target_pairs={{16,32},{32,16},{48,64},{64,48},{80,96},{96,80},{112,128},{128,112... | collective-permute-start | bytes 1769480 | tf_op jit(solution)/shard_map/ppermute | solution.py:308
  26.8 18.0 %collective-permute-start.7 = (f32[6,96,256]{2,1,0:T(8,128)S(1)}, f32[6,96,256]{2,1,0:T(8,128)S(1)}, u32[]{:S(2)}, u32[]{:S(2)}) collective-permute-start(f32[6,96,256]{2,1,0:T(8,128)S(1)} %get-tuple-element.44.refs_1_), channel_id=1, source_target_pairs={{0,16},{16,0},{32,48},{48,32},{64,80},{80,64},{96,112},{112,96},{1... | collective-permute-start | bytes 1769480 | tf_op jit(solution)/shard_map/ppermute | solution.py:308
  28.8 16.1 %copy-start.2 = (bf16[512,256]{1,0:T(8,128)(2,1)S(1)}, bf16[512,256]{1,0:T(8,128)(2,1)}, u32[]{:S(2)}) copy-start(bf16[512,256]{1,0:T(8,128)(2,1)} %constant.8.clone.refs_8_) | copy-start | bytes 786436
  32.6 21.9 %collective-permute-start.2 = (f32[6,96,256]{2,1,0:T(8,128)S(1)}, f32[6,96,256]{2,1,0:T(8,128)S(1)}, u32[]{:S(2)}, u32[]{:S(2)}) collective-permute-start(f32[6,96,256]{2,1,0:T(8,128)S(1)} %get-tuple-element.36.refs_1_), channel_id=1, source_target_pairs={{16,32},{32,16},{48,64},{64,48},{80,96},{96,80},{112,128},{128,112... | collective-permute-start | bytes 1769480 | tf_op jit(solution)/shard_map/ppermute | solution.py:308
  38.3 18.8 %collective-permute-start.3 = (f32[6,96,256]{2,1,0:T(8,128)S(1)}, f32[6,96,256]{2,1,0:T(8,128)S(1)}, u32[]{:S(2)}, u32[]{:S(2)}) collective-permute-start(f32[6,96,256]{2,1,0:T(8,128)S(1)} %get-tuple-element.36.refs_1_), channel_id=1, source_target_pairs={{0,16},{16,0},{32,48},{48,32},{64,80},{80,64},{96,112},{112,96},{1... | collective-permute-start | bytes 1769480 | tf_op jit(solution)/shard_map/ppermute | solution.py:308

commit v3 on v2

--- a/solution.py
+++ b/solution.py
@@ -194,7 +194,7 @@
                 conv[r, rows, lanes] = totals[n]
         return carry
 
-    lax.fori_loop(0, C // 8, conv_tile, 0)
+    lax.fori_loop(0, C // 8, conv_tile, 0, unroll=3)
     if not ends:
         tail(count, 0, field, conv, mixers, matrix, gain, parts, field_out, next_out)
         return

time: 61.7 us -> 63.1 us (1.023)
  Pallas kernels: 23.7 us -> 26.4 us
  waiting for transfers between devices: 12.6 us -> 11.2 us
    ppermute x8, waiting for transfers between devices: 12.6 us -> 11.2 us  [swap(): return lax.ppermute(own, axis, pairs)]
    pallas_call x2, Pallas kernels: 8.58 us -> 9.94 us  [last_pass(): pl.pallas_call(functools.partial(lattice_kernel, axis, True, part), grid=...]
    pallas_call x2, Pallas kernels: 7.52 us -> 8.87 us  [lattice_pass(): pl.pallas_call(functools.partial(lattice_kernel, axis, False, 0), grid=(1...]
  transfers between devices with their start and end apart: 8 -> 8, of which waited for: 4 -> 4; matrix products, arithmetic and copies ran while one was open for 0% -> 0% of each run, Pallas kernels for 28% -> 30%
where the time goes in v3:
time: 63.1 us; the launch traced here: 62.8 us
  Pallas kernels  26.4 us (42%)
  starting transfers between devices  24.8 us (39%)
  waiting for transfers between devices  11.2 us (18%)
    ppermute x8, starting transfers between devices, swap(): return lax.ppermute(own, axis, pairs)  24.8 us
    ppermute x8, waiting for transfers between devices, swap(): return lax.ppermute(own, axis, pairs)  11.2 us
    pallas_call x2, Pallas kernels, last_pass(): pl.pallas_call(functools.partial(lattice_kernel, axis, True, part), grid=...  9.94 us
    pallas_call x2, Pallas kernels, lattice_pass(): pl.pallas_call(functools.partial(lattice_kernel, axis, False, 0), grid=(1...  8.87 us
    pallas_call x2, Pallas kernels, rounds_pass(): pl.pallas_call(functools.partial(rounds_kernel, first), grid=(1,), in_spe...  5.13 us
    pallas_call x3, Pallas kernels, tap_tables(): pl.pallas_call(functools.partial(tables_kernel, kinds), grid=(1,), in_spe...  2.49 us
  transfers between devices with their start and end apart: 8, of which 4 were waited for; matrix products, arithmetic and copies ran while one was open for 0% of the time, Pallas kernels for 30%

profile of v3, /device:TPU:222, one launch (start us, length us, event | category | flops | bytes accessed | tf_op | source)
XLA Modules:
  0.0 62.8 jit_solution(3594892080840374265)
XLA Ops:
  0.0 2.4 %shard_map.110 = (f32[6,96,256]{2,1,0:T(8,128)S(1)}, f32[6,96,256]{2,1,0:T(8,128)S(1)}) custom-call(f32[12,96,256]{2,1,0:T(8,128)} %state_in.3, s32[8,256]{1,0:T(8,128)} %events_in.3, f32[1,96]{1,0:T(1,128)} %bitcast.10, f32[3,96]{1,0:T(4,128)} %refs_4_.7, f32[9,96]{1,0:T(8,128)} %bitcast.8, f32[3,2,96,96]{3,2,1,0:T(8,128)} %refs_7_.7, ...), custom_call_target="tpu_custom_call" | custom-call | flops 20000000 | bytes 100000 | tf_op jit(solution)/shard_map/pallas_call | solution.py:233
  2.4 0.0 copy-start
  2.4 0.0 copy-start.1
  2.5 2.1 %collective-permute-start.4 = (f32[6,96,256]{2,1,0:T(8,128)S(1)}, f32[6,96,256]{2,1,0:T(8,128)S(1)}, u32[]{:S(2)}, u32[]{:S(2)}) collective-permute-start(f32[6,96,256]{2,1,0:T(8,128)S(1)} %get-tuple-element.38.refs_1_), channel_id=1, source_target_pairs={{1,2},{2,1},{3,4},{4,3},{5,6},{6,5},{7,8},{8,7},{9,10},{10,9},{11,... | collective-permute-start | bytes 1769480 | tf_op jit(solution)/shard_map/ppermute | solution.py:308
  4.5 0.8 %shard_map.111 = (f32[16,96,128]{2,1,0:T(8,128)S(1)}, f32[17,96,128]{2,1,0:T(8,128)S(1)}) custom-call(f32[33,96]{1,0:T(8,128)S(1)} %bitcast.7), custom_call_target="tpu_custom_call" | custom-call | flops 1000000 | bytes 100000 | tf_op jit(solution)/shard_map/pallas_call | solution.py:259
  5.4 4.8 %collective-permute-start.5 = (f32[6,96,256]{2,1,0:T(8,128)S(1)}, f32[6,96,256]{2,1,0:T(8,128)S(1)}, u32[]{:S(2)}, u32[]{:S(2)}) collective-permute-start(f32[6,96,256]{2,1,0:T(8,128)S(1)} %get-tuple-element.38.refs_1_), channel_id=1, source_target_pairs={{0,1},{1,0},{2,3},{3,2},{4,5},{5,4},{6,7},{7,6},{8,9},{9,8},{10,11... | collective-permute-start | bytes 1769480 | tf_op jit(solution)/shard_map/ppermute | solution.py:308
  10.2 2.7 %shard_map.109 = (f32[6,96,256]{2,1,0:T(8,128)S(1)}, f32[6,96,256]{2,1,0:T(8,128)S(1)}) custom-call(f32[12,96,256]{2,1,0:T(8,128)} %state_in.3, s32[8,256]{1,0:T(8,128)} %events_in.3, f32[1,96]{1,0:T(1,128)} %bitcast.11, f32[3,96]{1,0:T(4,128)} %refs_4_.7, f32[9,96]{1,0:T(8,128)} %bitcast.9, f32[3,2,96,96]{3,2,1,0:T(8,128)} %refs_7_.7, ...), custom_call_target="tpu_custom_call" | custom-call | flops 20000000 | bytes 100000 | tf_op jit(solution)/shard_map/pallas_call | solution.py:233
  12.9 1.9 %collective-permute-start.1 = (f32[6,96,256]{2,1,0:T(8,128)S(1)}, f32[6,96,256]{2,1,0:T(8,128)S(1)}, u32[]{:S(2)}, u32[]{:S(2)}) collective-permute-start(f32[6,96,256]{2,1,0:T(8,128)S(1)} %get-tuple-element.26.refs_1_), channel_id=1, source_target_pairs={{0,1},{1,0},{2,3},{3,2},{4,5},{5,4},{6,7},{7,6},{8,9},{9,8},{10,11... | collective-permute-start | bytes 1769480 | tf_op jit(solution)/shard_map/ppermute | solution.py:308
  14.8 1.9 %collective-permute-start = (f32[6,96,256]{2,1,0:T(8,128)S(1)}, f32[6,96,256]{2,1,0:T(8,128)S(1)}, u32[]{:S(2)}, u32[]{:S(2)}) collective-permute-start(f32[6,96,256]{2,1,0:T(8,128)S(1)} %get-tuple-element.26.refs_1_), channel_id=1, source_target_pairs={{1,2},{2,1},{3,4},{4,3},{5,6},{6,5},{7,8},{8,7},{9,10},{10,9},{11,... | collective-permute-start | bytes 1769480 | tf_op jit(solution)/shard_map/ppermute | solution.py:308
  16.8 4.4 %shard_map.114 = (f32[6,96,256]{2,1,0:T(8,128)S(1)}, f32[6,96,256]{2,1,0:T(8,128)S(1)}) custom-call(f32[6,96,256]{2,1,0:T(8,128)S(1)} %get-tuple-element.37.refs_0_, f32[6,96,256]{2,1,0:T(8,128)S(1)} %get-tuple-element.38.refs_1_, f32[6,96,256]{2,1,0:T(8,128)S(1)} %collective-permute-done.4.refs_2_, f32[6,96,256]{2,1,0:T(8,128)S(1)} %collective-permute-done.5.refs_3_, ...), custom_call_target="tpu_custom_call" | custom-call | flops 1200000000 | bytes 100000 | tf_op jit(solution)/shard_map/pallas_call | solution.py:272
  21.3 5.4 %collective-permute-start.6 = (f32[6,96,256]{2,1,0:T(8,128)S(1)}, f32[6,96,256]{2,1,0:T(8,128)S(1)}, u32[]{:S(2)}, u32[]{:S(2)}) collective-permute-start(f32[6,96,256]{2,1,0:T(8,128)S(1)} %get-tuple-element.44.refs_1_), channel_id=1, source_target_pairs={{16,32},{32,16},{48,64},{64,48},{80,96},{96,80},{112,128},{128,112... | collective-permute-start | bytes 1769480 | tf_op jit(solution)/shard_map/ppermute | solution.py:308
  26.7 0.8 %shard_map.115.refs_5_ = f32[16,96,128]{2,1,0:T(8,128)S(1)} custom-call(f32[33,96]{1,0:T(8,128)S(1)} %bitcast.5), custom_call_target="tpu_custom_call" | custom-call | flops 1000000 | bytes 100000 | tf_op jit(solution)/shard_map/pallas_call | solution.py:259
  27.5 1.9 %collective-permute-start.7 = (f32[6,96,256]{2,1,0:T(8,128)S(1)}, f32[6,96,256]{2,1,0:T(8,128)S(1)}, u32[]{:S(2)}, u32[]{:S(2)}) collective-permute-start(f32[6,96,256]{2,1,0:T(8,128)S(1)} %get-tuple-element.44.refs_1_), channel_id=1, source_target_pairs={{0,16},{16,0},{32,48},{48,32},{64,80},{80,64},{96,112},{112,96},{1... | collective-permute-start | bytes 1769480 | tf_op jit(solution)/shard_map/ppermute | solution.py:308
  29.5 0.0 copy-start.2
  29.5 4.4 %shard_map.112 = (f32[6,96,256]{2,1,0:T(8,128)S(1)}, f32[6,96,256]{2,1,0:T(8,128)S(1)}) custom-call(f32[6,96,256]{2,1,0:T(8,128)S(1)} %get-tuple-element.25.refs_0_, f32[6,96,256]{2,1,0:T(8,128)S(1)} %get-tuple-element.26.refs_1_, f32[6,96,256]{2,1,0:T(8,128)S(1)} %collective-permute-done.refs_2_, f32[6,96,256]{2,1,0:T(8,128)S(1)} %collective-permute-done.1.refs_3_, ...), custom_call_target="tpu_custom_call" | custom-call | flops 1200000000 | bytes 100000 | tf_op jit(solution)/shard_map/pallas_call | solution.py:272
  33.9 4.9 %collective-permute-start.2 = (f32[6,96,256]{2,1,0:T(8,128)S(1)}, f32[6,96,256]{2,1,0:T(8,128)S(1)}, u32[]{:S(2)}, u32[]{:S(2)}) collective-permute-start(f32[6,96,256]{2,1,0:T(8,128)S(1)} %get-tuple-element.36.refs_1_), channel_id=1, source_target_pairs={{16,32},{32,16},{48,64},{64,48},{80,96},{96,80},{112,128},{128,112... | collective-permute-start | bytes 1769480 | tf_op jit(solution)/shard_map/ppermute | solution.py:308
  38.8 0.8 %shard_map.113.refs_6_ = f32[17,96,128]{2,1,0:T(8,128)S(1)} custom-call(f32[33,96]{1,0:T(8,128)S(1)} %bitcast.6), custom_call_target="tpu_custom_call" | custom-call | flops 1000000 | bytes 100000 | tf_op jit(solution)/shard_map/pallas_call | solution.py:259
  39.7 1.9 %collective-permute-start.3 = (f32[6,96,256]{2,1,0:T(8,128)S(1)}, f32[6,96,256]{2,1,0:T(8,128)S(1)}, u32[]{:S(2)}, u32[]{:S(2)}) collective-permute-start(f32[6,96,256]{2,1,0:T(8,128)S(1)} %get-tuple-element.36.refs_1_), channel_id=1, source_target_pairs={{0,16},{16,0},{32,48},{48,32},{64,80},{80,64},{96,112},{112,96},{1... | collective-permute-start | bytes 1769480 | tf_op jit(solution)/shard_map/ppermute | solution.py:308
  41.6 1.1 %collective-permute-done.6.refs_2_ = f32[6,96,256]{2,1,0:T(8,128)S(1)} collective-permute-done((f32[6,96,256]{2,1,0:T(8,128)S(1)}, f32[6,96,256]{2,1,0:T(8,128)S(1)}, u32[]{:S(2)}, u32[]{:S(2)}) %collective-permute-start.6) | collective-permute-done | bytes 589856 | tf_op jit(solution)/shard_map/ppermute | solution.py:308
  42.7 2.8 %collective-permute-done.7.refs_3_ = f32[6,96,256]{2,1,0:T(8,128)S(1)} collective-permute-done((f32[6,96,256]{2,1,0:T(8,128)S(1)}, f32[6,96,256]{2,1,0:T(8,128)S(1)}, u32[]{:S(2)}, u32[]{:S(2)}) %collective-permute-start.7) | collective-permute-done | bytes 589856 | tf_op jit(solution)/shard_map/ppermute | solution.py:308
  45.5 5.0 %shard_map.116.refs_9_ = f32[12,96,256]{2,1,0:T(8,128)} custom-call(f32[6,96,256]{2,1,0:T(8,128)S(1)} %get-tuple-element.43.refs_0_, f32[6,96,256]{2,1,0:T(8,128)S(1)} %get-tuple-element.44.refs_1_, f32[6,96,256]{2,1,0:T(8,128)S(1)} %collective-permute-done.6.refs_2_, f32[6,96,256]{2,1,0:T(8,128)S(1)} %collective-permute-done.7.refs_3_, ...), custom_call_target="tpu_custom_call" | custom-call | flops 1200000000 | bytes 100000 | tf_op jit(solution)/shard_map/pallas_call | solution.py:292
  50.5 4.6 %collective-permute-done.2.refs_2_ = f32[6,96,256]{2,1,0:T(8,128)S(1)} collective-permute-done((f32[6,96,256]{2,1,0:T(8,128)S(1)}, f32[6,96,256]{2,1,0:T(8,128)S(1)}, u32[]{:S(2)}, u32[]{:S(2)}) %collective-permute-start.2) | collective-permute-done | bytes 589856 | tf_op jit(solution)/shard_map/ppermute | solution.py:308
  55.1 2.7 %collective-permute-done.3.refs_3_ = f32[6,96,256]{2,1,0:T(8,128)S(1)} collective-permute-done((f32[6,96,256]{2,1,0:T(8,128)S(1)}, f32[6,96,256]{2,1,0:T(8,128)S(1)}, u32[]{:S(2)}, u32[]{:S(2)}) %collective-permute-start.3) | collective-permute-done | bytes 589856 | tf_op jit(solution)/shard_map/ppermute | solution.py:308
  57.8 5.0 %shard_map.117 = f32[12,96,256]{2,1,0:T(8,128)} custom-call(f32[6,96,256]{2,1,0:T(8,128)S(1)} %get-tuple-element.33.refs_0_, f32[6,96,256]{2,1,0:T(8,128)S(1)} %get-tuple-element.36.refs_1_, f32[6,96,256]{2,1,0:T(8,128)S(1)} %collective-permute-done.2.refs_2_, f32[6,96,256]{2,1,0:T(8,128)S(1)} %collective-permute-done.3.refs_3_, ...), custom_call_target="tpu_custom_call", output_to_operand_aliasing={{}: (9, {})} | custom-call | flops 1200000000 | bytes 100000 | tf_op jit(solution)/shard_map/pallas_call | solution.py:292
  (13 shorter events, 0.0 us)
Async XLA Ops:
  0.0 4.5 %copy-start.5 = (f32[96,33]{0,1:T(8,128)S(1)}, f32[96,33]{0,1:T(8,128)}, u32[]{:S(2)}) copy-start(f32[96,33]{0,1:T(8,128)} %param.16) | copy-start | bytes 38020
  2.4 14.4 %copy-start = (f32[3,2,96,96]{3,2,1,0:T(8,128)S(1)}, f32[3,2,96,96]{3,2,1,0:T(8,128)}, u32[]{:S(2)}) copy-start(f32[3,2,96,96]{3,2,1,0:T(8,128)} %refs_7_.7) | copy-start | bytes 663556
  2.4 14.4 %copy-start.1 = (bf16[512,256]{1,0:T(8,128)(2,1)S(1)}, bf16[512,256]{1,0:T(8,128)(2,1)}, u32[]{:S(2)}) copy-start(bf16[512,256]{1,0:T(8,128)(2,1)} %constant.7.clone.refs_8_) | copy-start | bytes 786436
  2.4 14.4 %copy-start.4 = (f32[3,96]{1,0:T(4,128)S(1)}, f32[3,96]{1,0:T(4,128)}, u32[]{:S(2)}) copy-start(f32[3,96]{1,0:T(4,128)} %refs_4_.7) | copy-start | bytes 3460
  2.5 14.3 %collective-permute-start.4 = (f32[6,96,256]{2,1,0:T(8,128)S(1)}, f32[6,96,256]{2,1,0:T(8,128)S(1)}, u32[]{:S(2)}, u32[]{:S(2)}) collective-permute-start(f32[6,96,256]{2,1,0:T(8,128)S(1)} %get-tuple-element.38.refs_1_), channel_id=1, source_target_pairs={{1,2},{2,1},{3,4},{4,3},{5,6},{6,5},{7,8},{8,7},{9,10},{10,9},{11,... | collective-permute-start | bytes 1769480 | tf_op jit(solution)/shard_map/ppermute | solution.py:308
  5.4 11.4 %collective-permute-start.5 = (f32[6,96,256]{2,1,0:T(8,128)S(1)}, f32[6,96,256]{2,1,0:T(8,128)S(1)}, u32[]{:S(2)}, u32[]{:S(2)}) collective-permute-start(f32[6,96,256]{2,1,0:T(8,128)S(1)} %get-tuple-element.38.refs_1_), channel_id=1, source_target_pairs={{0,1},{1,0},{2,3},{3,2},{4,5},{5,4},{6,7},{7,6},{8,9},{9,8},{10,11... | collective-permute-start | bytes 1769480 | tf_op jit(solution)/shard_map/ppermute | solution.py:308
  12.9 16.5 %collective-permute-start.1 = (f32[6,96,256]{2,1,0:T(8,128)S(1)}, f32[6,96,256]{2,1,0:T(8,128)S(1)}, u32[]{:S(2)}, u32[]{:S(2)}) collective-permute-start(f32[6,96,256]{2,1,0:T(8,128)S(1)} %get-tuple-element.26.refs_1_), channel_id=1, source_target_pairs={{0,1},{1,0},{2,3},{3,2},{4,5},{5,4},{6,7},{7,6},{8,9},{9,8},{10,11... | collective-permute-start | bytes 1769480 | tf_op jit(solution)/shard_map/ppermute | solution.py:308
  14.8 14.6 %collective-permute-start = (f32[6,96,256]{2,1,0:T(8,128)S(1)}, f32[6,96,256]{2,1,0:T(8,128)S(1)}, u32[]{:S(2)}, u32[]{:S(2)}) collective-permute-start(f32[6,96,256]{2,1,0:T(8,128)S(1)} %get-tuple-element.26.refs_1_), channel_id=1, source_target_pairs={{1,2},{2,1},{3,4},{4,3},{5,6},{6,5},{7,8},{8,7},{9,10},{10,9},{11,... | collective-permute-start | bytes 1769480 | tf_op jit(solution)/shard_map/ppermute | solution.py:308
  16.8 9.9 %copy-start.3 = (f32[96,33]{0,1:T(8,128)S(1)}, f32[96,33]{0,1:T(8,128)}, u32[]{:S(2)}) copy-start(f32[96,33]{0,1:T(8,128)} %param.17) | copy-start | bytes 38020
  21.3 21.4 %collective-permute-start.6 = (f32[6,96,256]{2,1,0:T(8,128)S(1)}, f32[6,96,256]{2,1,0:T(8,128)S(1)}, u32[]{:S(2)}, u32[]{:S(2)}) collective-permute-start(f32[6,96,256]{2,1,0:T(8,128)S(1)} %get-tuple-element.44.refs_1_), channel_id=1, source_target_pairs={{16,32},{32,16},{48,64},{64,48},{80,96},{96,80},{112,128},{128,112... | collective-permute-start | bytes 1769480 | tf_op jit(solution)/shard_map/ppermute | solution.py:308
  27.5 18.0 %collective-permute-start.7 = (f32[6,96,256]{2,1,0:T(8,128)S(1)}, f32[6,96,256]{2,1,0:T(8,128)S(1)}, u32[]{:S(2)}, u32[]{:S(2)}) collective-permute-start(f32[6,96,256]{2,1,0:T(8,128)S(1)} %get-tuple-element.44.refs_1_), channel_id=1, source_target_pairs={{0,16},{16,0},{32,48},{48,32},{64,80},{80,64},{96,112},{112,96},{1... | collective-permute-start | bytes 1769480 | tf_op jit(solution)/shard_map/ppermute | solution.py:308
  29.5 16.1 %copy-start.2 = (bf16[512,256]{1,0:T(8,128)(2,1)S(1)}, bf16[512,256]{1,0:T(8,128)(2,1)}, u32[]{:S(2)}) copy-start(bf16[512,256]{1,0:T(8,128)(2,1)} %constant.8.clone.refs_8_) | copy-start | bytes 786436
  33.9 21.2 %collective-permute-start.2 = (f32[6,96,256]{2,1,0:T(8,128)S(1)}, f32[6,96,256]{2,1,0:T(8,128)S(1)}, u32[]{:S(2)}, u32[]{:S(2)}) collective-permute-start(f32[6,96,256]{2,1,0:T(8,128)S(1)} %get-tuple-element.36.refs_1_), channel_id=1, source_target_pairs={{16,32},{32,16},{48,64},{64,48},{80,96},{96,80},{112,128},{128,112... | collective-permute-start | bytes 1769480 | tf_op jit(solution)/shard_map/ppermute | solution.py:308
  39.7 18.1 %collective-permute-start.3 = (f32[6,96,256]{2,1,0:T(8,128)S(1)}, f32[6,96,256]{2,1,0:T(8,128)S(1)}, u32[]{:S(2)}, u32[]{:S(2)}) collective-permute-start(f32[6,96,256]{2,1,0:T(8,128)S(1)} %get-tuple-element.36.refs_1_), channel_id=1, source_target_pairs={{0,16},{16,0},{32,48},{48,32},{64,80},{80,64},{96,112},{112,96},{1... | collective-permute-start | bytes 1769480 | tf_op jit(solution)/shard_map/ppermute | solution.py:308

commit v4 on v2

--- a/solution.py
+++ b/solution.py
@@ -77,16 +77,17 @@
     moved = dot(parts[...], matrix[...])
     for r in range(count):
         here = moved[r * C : (r + 1) * C]
-        field_out[r] = here
+        field_out[r // CHUNK][r % CHUNK] = here
         if sent is not None:
             sent(r)
         if next_out is not None:
-            next_out[r] = normed(here, gain)
+            next_out[r // CHUNK][r % CHUNK] = normed(here, gain)
 
 
 def rounds_kernel(
-    first, state_in, events_in, embed_in, gains_in, taps_in, mixers_in, matrix_in, field_out, next_out, *work
+    first, state_in, events_in, embed_in, gains_in, taps_in, mixers_in, matrix_in, *refs
 ):
+    outs, work = refs[: 2 * PARTS], refs[2 * PARTS :]
     ext, state, events, embed, gains, taps, mixers, matrix, conv, parts, sems = work
     last = state.shape[0]
     count = last - first
@@ -128,7 +129,7 @@
                 conv[r, rows, lanes] = total
     for copy in copies[4:]:
         copy.wait()
-    tail(count, first, state, conv, mixers, matrix, gain_next, parts, field_out, next_out)
+    tail(count, first, state, conv, mixers, matrix, gain_next, parts, outs[0::2], outs[1::2])
 
 
 def tables_kernel(kinds, taps, *tables):
@@ -196,13 +197,13 @@
 
     lax.fori_loop(0, C // 8, conv_tile, 0)
     if not ends:
-        tail(count, 0, field, conv, mixers, matrix, gain, parts, field_out, next_out)
+        tail(count, 0, field, conv, mixers, matrix, gain, parts, [field_out], [next_out])
         return
 
     copies = [
         pltpu.make_async_copy(conv.at[r], result.at[part * CHUNK + r], sems.at[r]) for r in range(count)
     ]
-    tail(count, 0, field, conv, mixers, matrix, None, parts, conv, None, lambda r: copies[r].start())
+    tail(count, 0, field, conv, mixers, matrix, None, parts, [conv], None, lambda r: copies[r].start())
     for copy in copies:
         copy.wait()
 
@@ -221,15 +222,15 @@
 
 PARAMS = pltpu.CompilerParams(vmem_limit_bytes=VMEM)
 BLOCK = (CHUNK, C, SITES)
+PARTS = ROUNDS // CHUNK
 FULL = (ROUNDS, C, SITES)
 WORK = [pltpu.VMEM(BLOCK, jnp.float32), pltpu.VMEM((CHUNK * C, 2 * SITES), jnp.bfloat16)]
 
 
-def rounds_pass(part, inputs):
+def rounds_pass(inputs):
     state, events, embed, gains, taps, mixers, matrix = inputs
-    first = part * CHUNK
-    last = first + CHUNK
-    outs = [BLOCK, BLOCK]
+    first, last = 0, ROUNDS
+    outs = [BLOCK, BLOCK] * PARTS
     return pl.pallas_call(
         functools.partial(rounds_kernel, first),
         grid=(1,),
@@ -246,7 +247,7 @@
             pltpu.VMEM((1,) + mixers.shape[1:], jnp.float32),
             pltpu.VMEM(matrix.shape, jnp.bfloat16),
         ]
-        + WORK
+        + [pltpu.VMEM(FULL, jnp.float32), pltpu.VMEM((ROUNDS * C, 2 * SITES), jnp.bfloat16)]
         + [pltpu.SemaphoreType.DMA((last + 6,))],
         compiler_params=PARAMS,
         cost_estimate=cost(20_000_000),
@@ -318,11 +319,10 @@
         for a in (state, events, event_embed[None, :], gains, taps_t.T, mixers, to_y)
     ]
 
-    field_a, own_a = rounds_pass(0, inputs)
+    field_a, own_a, field_b, own_b = rounds_pass(inputs)
     odd_a = swap(own_a, "gy", 1)
     table_y, held = lax.optimization_barrier((tap_tables(("own", "far"), taps_y, own_a), own_a))
     even_a = swap(held, "gy", 0)
-    field_b, own_b = rounds_pass(1, inputs)
     odd_b = swap(own_b, "gy", 1)
     even_b = swap(own_b, "gy", 0)
     field_a, own_a = lattice_pass("gy", field_a, own_a, (odd_a, even_a), gains, table_y, mixers, to_x)

time: 61.7 us -> 60.3 us (0.977)
  Pallas kernels: 23.7 us -> 22.3 us
    pallas_call x2 -> x1, Pallas kernels: 5.13 us -> 3.7 us  [rounds_pass(): pl.pallas_call(functools.partial(rounds_kernel, first), grid=(1,), in_spe...]
  transfers between devices with their start and end apart: 8 -> 8, of which waited for: 4 -> 4; matrix products, arithmetic and copies ran while one was open for 0% -> 0% of each run, Pallas kernels for 28% -> 24%
where the time goes in v4:
time: 60.3 us; the launch traced here: 59.9 us
  starting transfers between devices  24.7 us (41%)
  Pallas kernels  22.3 us (37%)
  waiting for transfers between devices  12.7 us (21%)
    ppermute x8, starting transfers between devices, swap(): return lax.ppermute(own, axis, pairs)  24.7 us
    ppermute x8, waiting for transfers between devices, swap(): return lax.ppermute(own, axis, pairs)  12.7 us
    pallas_call x2, Pallas kernels, last_pass(): pl.pallas_call(functools.partial(lattice_kernel, axis, True, part), grid=...  8.58 us
    pallas_call x2, Pallas kernels, lattice_pass(): pl.pallas_call(functools.partial(lattice_kernel, axis, False, 0), grid=(1...  7.52 us
    pallas_call x1, Pallas kernels, rounds_pass(): pl.pallas_call(functools.partial(rounds_kernel, first), grid=(1,), in_spe...  3.7 us
    pallas_call x3, Pallas kernels, tap_tables(): pl.pallas_call(functools.partial(tables_kernel, kinds), grid=(1,), in_spe...  2.49 us
  transfers between devices with their start and end apart: 8, of which 4 were waited for; matrix products, arithmetic and copies ran while one was open for 0% of the time, Pallas kernels for 24%

profile of v4, /device:TPU:222, one launch (start us, length us, event | category | flops | bytes accessed | tf_op | source)
XLA Modules:
  0.0 59.9 jit_solution(3399478210947917540)
XLA Ops:
  0.0 3.7 %shard_map.109 = (f32[6,96,256]{2,1,0:T(8,128)S(1)}, f32[6,96,256]{2,1,0:T(8,128)S(1)}, f32[6,96,256]{2,1,0:T(8,128)S(1)}, f32[6,96,256]{2,1,0:T(8,128)S(1)}) custom-call(f32[12,96,256]{2,1,0:T(8,128)} %state_in.1, s32[8,256]{1,0:T(8,128)} %events_in.1, f32[1,96]{1,0:T(1,128)} %bitcast.9, f32[3,96]{1,0:T(4,128)} %refs_4_.7, f32[9,96]{1,0:T(8,128)} %bitcast.8, ...), custom_call_target="tpu_custom_call" | custom-call | flops 20000000 | bytes 100000 | tf_op jit(solution)/shard_map/pallas_call | solution.py:234
  3.7 1.9 %collective-permute-start.4 = (f32[6,96,256]{2,1,0:T(8,128)S(1)}, f32[6,96,256]{2,1,0:T(8,128)S(1)}, u32[]{:S(2)}, u32[]{:S(2)}) collective-permute-start(f32[6,96,256]{2,1,0:T(8,128)S(1)} %get-tuple-element.38.refs_1_), channel_id=1, source_target_pairs={{1,2},{2,1},{3,4},{4,3},{5,6},{6,5},{7,8},{8,7},{9,10},{10,9},{11,... | collective-permute-start | bytes 1769480 | tf_op jit(solution)/shard_map/ppermute | solution.py:309
  5.7 0.8 %shard_map.110 = (f32[16,96,128]{2,1,0:T(8,128)S(1)}, f32[17,96,128]{2,1,0:T(8,128)S(1)}) custom-call(f32[33,96]{1,0:T(8,128)S(1)} %bitcast.7), custom_call_target="tpu_custom_call" | custom-call | flops 1000000 | bytes 100000 | tf_op jit(solution)/shard_map/pallas_call | solution.py:260
  6.5 4.8 %collective-permute-start.5 = (f32[6,96,256]{2,1,0:T(8,128)S(1)}, f32[6,96,256]{2,1,0:T(8,128)S(1)}, u32[]{:S(2)}, u32[]{:S(2)}) collective-permute-start(f32[6,96,256]{2,1,0:T(8,128)S(1)} %get-tuple-element.38.refs_1_), channel_id=1, source_target_pairs={{0,1},{1,0},{2,3},{3,2},{4,5},{5,4},{6,7},{7,6},{8,9},{9,8},{10,11... | collective-permute-start | bytes 1769480 | tf_op jit(solution)/shard_map/ppermute | solution.py:309
  11.3 1.9 %collective-permute-start.1 = (f32[6,96,256]{2,1,0:T(8,128)S(1)}, f32[6,96,256]{2,1,0:T(8,128)S(1)}, u32[]{:S(2)}, u32[]{:S(2)}) collective-permute-start(f32[6,96,256]{2,1,0:T(8,128)S(1)} %get-tuple-element.26.refs_1_), channel_id=1, source_target_pairs={{0,1},{1,0},{2,3},{3,2},{4,5},{5,4},{6,7},{7,6},{8,9},{9,8},{10,11... | collective-permute-start | bytes 1769480 | tf_op jit(solution)/shard_map/ppermute | solution.py:309
  13.2 1.9 %collective-permute-start = (f32[6,96,256]{2,1,0:T(8,128)S(1)}, f32[6,96,256]{2,1,0:T(8,128)S(1)}, u32[]{:S(2)}, u32[]{:S(2)}) collective-permute-start(f32[6,96,256]{2,1,0:T(8,128)S(1)} %get-tuple-element.26.refs_1_), channel_id=1, source_target_pairs={{1,2},{2,1},{3,4},{4,3},{5,6},{6,5},{7,8},{8,7},{9,10},{10,9},{11,... | collective-permute-start | bytes 1769480 | tf_op jit(solution)/shard_map/ppermute | solution.py:309
  15.2 0.0 collective-permute-done.4.refs_2_
  15.2 0.0 copy-start.3
  15.2 3.8 %shard_map.113 = (f32[6,96,256]{2,1,0:T(8,128)S(1)}, f32[6,96,256]{2,1,0:T(8,128)S(1)}) custom-call(f32[6,96,256]{2,1,0:T(8,128)S(1)} %get-tuple-element.37.refs_0_, f32[6,96,256]{2,1,0:T(8,128)S(1)} %get-tuple-element.38.refs_1_, f32[6,96,256]{2,1,0:T(8,128)S(1)} %collective-permute-done.4.refs_2_, f32[6,96,256]{2,1,0:T(8,128)S(1)} %collective-permute-done.5.refs_3_, ...), custom_call_target="tpu_custom_call" | custom-call | flops 1200000000 | bytes 100000 | tf_op jit(solution)/shard_map/pallas_call | solution.py:273
  19.0 5.4 %collective-permute-start.6 = (f32[6,96,256]{2,1,0:T(8,128)S(1)}, f32[6,96,256]{2,1,0:T(8,128)S(1)}, u32[]{:S(2)}, u32[]{:S(2)}) collective-permute-start(f32[6,96,256]{2,1,0:T(8,128)S(1)} %get-tuple-element.44.refs_1_), channel_id=1, source_target_pairs={{16,32},{32,16},{48,64},{64,48},{80,96},{96,80},{112,128},{128,112... | collective-permute-start | bytes 1769480 | tf_op jit(solution)/shard_map/ppermute | solution.py:309
  24.4 0.8 %shard_map.114.refs_5_ = f32[16,96,128]{2,1,0:T(8,128)S(1)} custom-call(f32[33,96]{1,0:T(8,128)S(1)} %bitcast.5), custom_call_target="tpu_custom_call" | custom-call | flops 1000000 | bytes 100000 | tf_op jit(solution)/shard_map/pallas_call | solution.py:260
  25.2 1.9 %collective-permute-start.7 = (f32[6,96,256]{2,1,0:T(8,128)S(1)}, f32[6,96,256]{2,1,0:T(8,128)S(1)}, u32[]{:S(2)}, u32[]{:S(2)}) collective-permute-start(f32[6,96,256]{2,1,0:T(8,128)S(1)} %get-tuple-element.44.refs_1_), channel_id=1, source_target_pairs={{0,16},{16,0},{32,48},{48,32},{64,80},{80,64},{96,112},{112,96},{1... | collective-permute-start | bytes 1769480 | tf_op jit(solution)/shard_map/ppermute | solution.py:309
  27.2 0.0 collective-permute-done.1.refs_3_
  27.2 0.0 copy-start.2
  27.2 3.8 %shard_map.111 = (f32[6,96,256]{2,1,0:T(8,128)S(1)}, f32[6,96,256]{2,1,0:T(8,128)S(1)}) custom-call(f32[6,96,256]{2,1,0:T(8,128)S(1)} %get-tuple-element.25.refs_0_, f32[6,96,256]{2,1,0:T(8,128)S(1)} %get-tuple-element.26.refs_1_, f32[6,96,256]{2,1,0:T(8,128)S(1)} %collective-permute-done.refs_2_, f32[6,96,256]{2,1,0:T(8,128)S(1)} %collective-permute-done.1.refs_3_, ...), custom_call_target="tpu_custom_call" | custom-call | flops 1200000000 | bytes 100000 | tf_op jit(solution)/shard_map/pallas_call | solution.py:273
  31.0 4.9 %collective-permute-start.2 = (f32[6,96,256]{2,1,0:T(8,128)S(1)}, f32[6,96,256]{2,1,0:T(8,128)S(1)}, u32[]{:S(2)}, u32[]{:S(2)}) collective-permute-start(f32[6,96,256]{2,1,0:T(8,128)S(1)} %get-tuple-element.36.refs_1_), channel_id=1, source_target_pairs={{16,32},{32,16},{48,64},{64,48},{80,96},{96,80},{112,128},{128,112... | collective-permute-start | bytes 1769480 | tf_op jit(solution)/shard_map/ppermute | solution.py:309
  35.9 0.8 %shard_map.112.refs_6_ = f32[17,96,128]{2,1,0:T(8,128)S(1)} custom-call(f32[33,96]{1,0:T(8,128)S(1)} %bitcast.6), custom_call_target="tpu_custom_call" | custom-call | flops 1000000 | bytes 100000 | tf_op jit(solution)/shard_map/pallas_call | solution.py:260
  36.7 1.9 %collective-permute-start.3 = (f32[6,96,256]{2,1,0:T(8,128)S(1)}, f32[6,96,256]{2,1,0:T(8,128)S(1)}, u32[]{:S(2)}, u32[]{:S(2)}) collective-permute-start(f32[6,96,256]{2,1,0:T(8,128)S(1)} %get-tuple-element.36.refs_1_), channel_id=1, source_target_pairs={{0,16},{16,0},{32,48},{48,32},{64,80},{80,64},{96,112},{112,96},{1... | collective-permute-start | bytes 1769480 | tf_op jit(solution)/shard_map/ppermute | solution.py:309
  38.6 1.8 %collective-permute-done.6.refs_2_ = f32[6,96,256]{2,1,0:T(8,128)S(1)} collective-permute-done((f32[6,96,256]{2,1,0:T(8,128)S(1)}, f32[6,96,256]{2,1,0:T(8,128)S(1)}, u32[]{:S(2)}, u32[]{:S(2)}) %collective-permute-start.6) | collective-permute-done | bytes 589856 | tf_op jit(solution)/shard_map/ppermute | solution.py:309
  40.4 2.8 %collective-permute-done.7.refs_3_ = f32[6,96,256]{2,1,0:T(8,128)S(1)} collective-permute-done((f32[6,96,256]{2,1,0:T(8,128)S(1)}, f32[6,96,256]{2,1,0:T(8,128)S(1)}, u32[]{:S(2)}, u32[]{:S(2)}) %collective-permute-start.7) | collective-permute-done | bytes 589856 | tf_op jit(solution)/shard_map/ppermute | solution.py:309
  43.3 4.3 %shard_map.115.refs_9_ = f32[12,96,256]{2,1,0:T(8,128)} custom-call(f32[6,96,256]{2,1,0:T(8,128)S(1)} %get-tuple-element.43.refs_0_, f32[6,96,256]{2,1,0:T(8,128)S(1)} %get-tuple-element.44.refs_1_, f32[6,96,256]{2,1,0:T(8,128)S(1)} %collective-permute-done.6.refs_2_, f32[6,96,256]{2,1,0:T(8,128)S(1)} %collective-permute-done.7.refs_3_, ...), custom_call_target="tpu_custom_call" | custom-call | flops 1200000000 | bytes 100000 | tf_op jit(solution)/shard_map/pallas_call | solution.py:293
  47.6 5.4 %collective-permute-done.2.refs_2_ = f32[6,96,256]{2,1,0:T(8,128)S(1)} collective-permute-done((f32[6,96,256]{2,1,0:T(8,128)S(1)}, f32[6,96,256]{2,1,0:T(8,128)S(1)}, u32[]{:S(2)}, u32[]{:S(2)}) %collective-permute-start.2) | collective-permute-done | bytes 589856 | tf_op jit(solution)/shard_map/ppermute | solution.py:309
  53.0 2.6 %collective-permute-done.3.refs_3_ = f32[6,96,256]{2,1,0:T(8,128)S(1)} collective-permute-done((f32[6,96,256]{2,1,0:T(8,128)S(1)}, f32[6,96,256]{2,1,0:T(8,128)S(1)}, u32[]{:S(2)}, u32[]{:S(2)}) %collective-permute-start.3) | collective-permute-done | bytes 589856 | tf_op jit(solution)/shard_map/ppermute | solution.py:309
  55.6 4.3 %shard_map.116 = f32[12,96,256]{2,1,0:T(8,128)} custom-call(f32[6,96,256]{2,1,0:T(8,128)S(1)} %get-tuple-element.33.refs_0_, f32[6,96,256]{2,1,0:T(8,128)S(1)} %get-tuple-element.36.refs_1_, f32[6,96,256]{2,1,0:T(8,128)S(1)} %collective-permute-done.2.refs_2_, f32[6,96,256]{2,1,0:T(8,128)S(1)} %collective-permute-done.3.refs_3_, ...), custom_call_target="tpu_custom_call", output_to_operand_aliasing={{}: (9, {})} | custom-call | flops 1200000000 | bytes 100000 | tf_op jit(solution)/shard_map/pallas_call | solution.py:293
  (12 shorter events, 0.0 us)
Async XLA Ops:
  0.0 15.2 %copy-start.1 = (bf16[512,256]{1,0:T(8,128)(2,1)S(1)}, bf16[512,256]{1,0:T(8,128)(2,1)}, u32[]{:S(2)}) copy-start(bf16[512,256]{1,0:T(8,128)(2,1)} %constant.7.clone.refs_8_) | copy-start | bytes 786436
  0.0 15.2 %copy-start = (f32[3,2,96,96]{3,2,1,0:T(8,128)S(1)}, f32[3,2,96,96]{3,2,1,0:T(8,128)}, u32[]{:S(2)}) copy-start(f32[3,2,96,96]{3,2,1,0:T(8,128)} %refs_7_.7) | copy-start | bytes 663556
  0.0 15.2 %copy-start.4 = (f32[3,96]{1,0:T(4,128)S(1)}, f32[3,96]{1,0:T(4,128)}, u32[]{:S(2)}) copy-start(f32[3,96]{1,0:T(4,128)} %refs_4_.7) | copy-start | bytes 3460
  0.0 5.6 %copy-start.5 = (f32[96,33]{0,1:T(8,128)S(1)}, f32[96,33]{0,1:T(8,128)}, u32[]{:S(2)}) copy-start(f32[96,33]{0,1:T(8,128)} %param.16) | copy-start | bytes 38020
  3.7 11.5 %collective-permute-start.4 = (f32[6,96,256]{2,1,0:T(8,128)S(1)}, f32[6,96,256]{2,1,0:T(8,128)S(1)}, u32[]{:S(2)}, u32[]{:S(2)}) collective-permute-start(f32[6,96,256]{2,1,0:T(8,128)S(1)} %get-tuple-element.38.refs_1_), channel_id=1, source_target_pairs={{1,2},{2,1},{3,4},{4,3},{5,6},{6,5},{7,8},{8,7},{9,10},{10,9},{11,... | collective-permute-start | bytes 1769480 | tf_op jit(solution)/shard_map/ppermute | solution.py:309
  6.5 8.7 %collective-permute-start.5 = (f32[6,96,256]{2,1,0:T(8,128)S(1)}, f32[6,96,256]{2,1,0:T(8,128)S(1)}, u32[]{:S(2)}, u32[]{:S(2)}) collective-permute-start(f32[6,96,256]{2,1,0:T(8,128)S(1)} %get-tuple-element.38.refs_1_), channel_id=1, source_target_pairs={{0,1},{1,0},{2,3},{3,2},{4,5},{5,4},{6,7},{7,6},{8,9},{9,8},{10,11... | collective-permute-start | bytes 1769480 | tf_op jit(solution)/shard_map/ppermute | solution.py:309
  11.3 15.9 %collective-permute-start.1 = (f32[6,96,256]{2,1,0:T(8,128)S(1)}, f32[6,96,256]{2,1,0:T(8,128)S(1)}, u32[]{:S(2)}, u32[]{:S(2)}) collective-permute-start(f32[6,96,256]{2,1,0:T(8,128)S(1)} %get-tuple-element.26.refs_1_), channel_id=1, source_target_pairs={{0,1},{1,0},{2,3},{3,2},{4,5},{5,4},{6,7},{7,6},{8,9},{9,8},{10,11... | collective-permute-start | bytes 1769480 | tf_op jit(solution)/shard_map/ppermute | solution.py:309
  13.2 13.9 %collective-permute-start = (f32[6,96,256]{2,1,0:T(8,128)S(1)}, f32[6,96,256]{2,1,0:T(8,128)S(1)}, u32[]{:S(2)}, u32[]{:S(2)}) collective-permute-start(f32[6,96,256]{2,1,0:T(8,128)S(1)} %get-tuple-element.26.refs_1_), channel_id=1, source_target_pairs={{1,2},{2,1},{3,4},{4,3},{5,6},{6,5},{7,8},{8,7},{9,10},{10,9},{11,... | collective-permute-start | bytes 1769480 | tf_op jit(solution)/shard_map/ppermute | solution.py:309
  15.2 9.2 %copy-start.3 = (f32[96,33]{0,1:T(8,128)S(1)}, f32[96,33]{0,1:T(8,128)}, u32[]{:S(2)}) copy-start(f32[96,33]{0,1:T(8,128)} %param.17) | copy-start | bytes 38020
  19.0 21.4 %collective-permute-start.6 = (f32[6,96,256]{2,1,0:T(8,128)S(1)}, f32[6,96,256]{2,1,0:T(8,128)S(1)}, u32[]{:S(2)}, u32[]{:S(2)}) collective-permute-start(f32[6,96,256]{2,1,0:T(8,128)S(1)} %get-tuple-element.44.refs_1_), channel_id=1, source_target_pairs={{16,32},{32,16},{48,64},{64,48},{80,96},{96,80},{112,128},{128,112... | collective-permute-start | bytes 1769480 | tf_op jit(solution)/shard_map/ppermute | solution.py:309
  25.2 18.0 %collective-permute-start.7 = (f32[6,96,256]{2,1,0:T(8,128)S(1)}, f32[6,96,256]{2,1,0:T(8,128)S(1)}, u32[]{:S(2)}, u32[]{:S(2)}) collective-permute-start(f32[6,96,256]{2,1,0:T(8,128)S(1)} %get-tuple-element.44.refs_1_), channel_id=1, source_target_pairs={{0,16},{16,0},{32,48},{48,32},{64,80},{80,64},{96,112},{112,96},{1... | collective-permute-start | bytes 1769480 | tf_op jit(solution)/shard_map/ppermute | solution.py:309
  27.2 16.1 %copy-start.2 = (bf16[512,256]{1,0:T(8,128)(2,1)S(1)}, bf16[512,256]{1,0:T(8,128)(2,1)}, u32[]{:S(2)}) copy-start(bf16[512,256]{1,0:T(8,128)(2,1)} %constant.8.clone.refs_8_) | copy-start | bytes 786436
  31.0 22.0 %collective-permute-start.2 = (f32[6,96,256]{2,1,0:T(8,128)S(1)}, f32[6,96,256]{2,1,0:T(8,128)S(1)}, u32[]{:S(2)}, u32[]{:S(2)}) collective-permute-start(f32[6,96,256]{2,1,0:T(8,128)S(1)} %get-tuple-element.36.refs_1_), channel_id=1, source_target_pairs={{16,32},{32,16},{48,64},{64,48},{80,96},{96,80},{112,128},{128,112... | collective-permute-start | bytes 1769480 | tf_op jit(solution)/shard_map/ppermute | solution.py:309
  36.7 18.9 %collective-permute-start.3 = (f32[6,96,256]{2,1,0:T(8,128)S(1)}, f32[6,96,256]{2,1,0:T(8,128)S(1)}, u32[]{:S(2)}, u32[]{:S(2)}) collective-permute-start(f32[6,96,256]{2,1,0:T(8,128)S(1)} %get-tuple-element.36.refs_1_), channel_id=1, source_target_pairs={{0,16},{16,0},{32,48},{48,32},{64,80},{80,64},{96,112},{112,96},{1... | collective-permute-start | bytes 1769480 | tf_op jit(solution)/shard_map/ppermute | solution.py:309
